TPU v7x, 32 devices: a whole 2x2x4 slice. The times are simulated.
32 devices in a mesh: gx: 8 (over y, x, core), yz: 4 (over z).
Axes of the slice: x: 2, y: 2, z: 4, core: 2. Of those that a mesh axis runs over, the one named last changes fastest.
Arguments:
- populations: bfloat16 [19, 128, 128, 128], P(None, 'gx', 'yz'), may hold values from -0.29882812 to 0.29882812
- levels: int32 [512], replicated, may hold values from 0 to 1
- refine_flags: int32 [512], replicated, may hold values from 0 to 2, as said below
- new_owner: int32 [512], replicated, may hold values from 0 to 31, as said below
Outputs:
- migrated: bfloat16 [768, 19, 4096], P(('gx', 'yz'))
Inputs may be any that keep to these rules, and one draw needn't show every extreme that they name: On every device exactly 8 of the blocks it holds have refine_flags 1 or 2; all other blocks have 0. `new_owner`: A block with refine_flags 0 keeps the device that holds it. No device receives more than one flagged block from any one device, itself included. After migration a quarter of the devices hold exactly 24 blocks, a quarter exactly 16, and the rest exactly 16 minus half of 8.
All inputs are finite; a program needn't handle non-finite values.
Results may differ from a plain program's by a relative error of at most 0.0049.
Values may be sent and summed in bfloat16 or wider, within the bound.
A program may use at most 192 MiB of HBM per device.

v0:
```python
import functools

import jax
import jax.numpy as jnp
import numpy as np
from jax import lax
from jax.experimental import pallas as pl
from jax.experimental.pallas import tpu as pltpu
from jax.sharding import PartitionSpec as P

BS = 16
HALF = 8
MIG = 8
CAP = 24
MESH = pl.DeviceIdType.MESH

VELOCITY = [
    (0, 0, 0),
    (1, 0, 0),
    (-1, 0, 0),
    (0, 1, 0),
    (0, -1, 0),
    (0, 0, 1),
    (0, 0, -1),
    (1, 1, 0),
    (-1, -1, 0),
    (1, -1, 0),
    (-1, 1, 0),
    (1, 0, 1),
    (-1, 0, -1),
    (1, 0, -1),
    (-1, 0, 1),
    (0, 1, 1),
    (0, -1, -1),
    (0, 1, -1),
    (0, -1, 1),
]
WEIGHT = [1.0 / 3.0] + [1.0 / 18.0] * 6 + [1.0 / 36.0] * 12
OPPOSITE = [0, 2, 1, 4, 3, 6, 5, 8, 7, 10, 9, 12, 11, 14, 13, 16, 15, 18, 17]
POPS = len(VELOCITY)
PAD = 8
FACES = [(1, 0), (-1, 0), (0, 1), (0, -1)]
CORNERS = [(1, 1), (-1, -1), (1, -1), (-1, 1)]
NEIGHBOURS = FACES + CORNERS
CROSSING = [
    [p for p in range(POPS) if VELOCITY[p][0] == 1],
    [p for p in range(POPS) if VELOCITY[p][0] == -1],
    [p for p in range(POPS) if VELOCITY[p][1] == 1],
    [p for p in range(POPS) if VELOCITY[p][1] == -1],
]


def total(terms):
    while len(terms) > 1:
        pairs = [a + b for a, b in zip(terms[::2], terms[1::2])]
        terms = pairs + ([terms[-1]] if len(terms) % 2 else [])
    return terms[0]


def collide(values, rate):
    edge = [values[p] for p in range(7, POPS)]
    density = 1.0 + (
        (1.0 / 3.0) * values[0] + (1.0 / 18.0) * total(values[1:7]) + (1.0 / 36.0) * total(edge)
    )
    inverse = 1.0 / density
    speeds = []
    for axis in range(3):
        face = None
        diagonal = None
        for p in range(1, POPS, 2):
            sign = VELOCITY[p][axis]
            if sign == 0:
                continue
            difference = values[p] - values[p + 1]
            if p < 7:
                face = difference if sign == 1 else -difference
            elif diagonal is None:
                diagonal = difference if sign == 1 else -difference
            else:
                diagonal = diagonal + difference if sign == 1 else diagonal - difference
        speeds.append(((1.0 / 18.0) * face + (1.0 / 36.0) * diagonal) * inverse)
    square = speeds[0] * speeds[0] + speeds[1] * speeds[1] + speeds[2] * speeds[2]
    keep = 1.0 - rate
    scaled = rate * density
    base = scaled * (1.0 - 1.5 * square) - rate
    results = [keep * values[0] + base]
    for p in range(1, POPS, 2):
        project = None
        for axis in range(3):
            sign = VELOCITY[p][axis]
            if sign == 0:
                continue
            if project is None:
                project = speeds[axis] if sign == 1 else -speeds[axis]
            else:
                project = project + speeds[axis] if sign == 1 else project - speeds[axis]
        even = base + scaled * (4.5 * project * project)
        odd = scaled * (3.0 * project)
        results.append(keep * values[p] + (even + odd))
        results.append(keep * values[p + 1] + (even - odd))
    return results


def steps_kernel(
    nx,
    ny,
    pop_ref,
    rate_ref,
    out_ref,
    first,
    second,
    x_send,
    x_recv,
    y_send,
    y_recv,
    c_send,
    c_recv,
    send_sem,
    recv_sem,
):
    nz = pop_ref.shape[3]
    gx = lax.axis_index("gx")
    yz = lax.axis_index("yz")
    gx_count = lax.axis_size("gx")
    yz_count = lax.axis_size("yz")

    def device(offset):
        return (
            lax.rem(gx + offset[0] + gx_count, gx_count),
            lax.rem(yz + offset[1] + yz_count, yz_count),
        )

    barrier = pltpu.get_barrier_semaphore()
    for offset in NEIGHBOURS:
        pl.semaphore_signal(barrier, inc=1, device_id=device(offset), device_id_type=MESH)
    lane = lax.broadcasted_iota(jnp.int32, (BS, nz), 1)

    def put(target, x, start, collided):
        for p in range(POPS):
            rounded = collided[p].astype(jnp.bfloat16).astype(jnp.float32)
            target[p, x + 1, PAD + start : PAD + start + BS, :] = rounded

    def gather(source, x, start):
        values = []
        for p in range(POPS):
            dx, dy, dz = VELOCITY[p]
            low = PAD + start - dy
            value = source[p, x + 1 - dx, low : low + BS, :]
            if dz != 0:
                mirror = source[OPPOSITE[p], x + 1, PAD + start : PAD + start + BS, :]
                if dz == 1:
                    value = jnp.where(lane == 0, mirror, pltpu.roll(value, 1, axis=1))
                else:
                    value = jnp.where(lane == nz - 1, mirror, pltpu.roll(value, nz - 1, axis=1))
            values.append(value)
        return values

    def exchange(step, field):
        for side in range(2):
            plane = nx if side == 0 else 1
            row = PAD + ny - 1 if side == 0 else PAD
            for k, p in enumerate(CROSSING[side]):
                x_send[step, side, k] = field[p, plane, PAD : PAD + ny, :]

        def pack(x, carry):
            for side in range(2):
                row = PAD + ny - 1 if side == 0 else PAD
                for k, p in enumerate(CROSSING[2 + side]):
                    y_send[step, side, k, pl.ds(x, 1), :] = field[p, x + 1, row : row + 1, :]
            return carry

        lax.fori_loop(0, nx, pack, 0)
        for c, (dx, dy) in enumerate(CORNERS):
            low = ny if dy == 1 else PAD
            c_send[step, c] = field[7 + c, nx if dx == 1 else 1, low : low + PAD, :]
        if step == 0:
            pl.semaphore_wait(barrier, len(NEIGHBOURS))
        copies = []
        for n, offset in enumerate(NEIGHBOURS):
            if n < 2:
                pair = (x_send.at[step, n], x_recv.at[step, n])
            elif n < 4:
                pair = (y_send.at[step, n - 2], y_recv.at[step, n - 2])
            else:
                pair = (c_send.at[step, n - 4], c_recv.at[step, n - 4])
            copy = pltpu.make_async_remote_copy(
                src_ref=pair[0],
                dst_ref=pair[1],
                send_sem=send_sem.at[step, n],
                recv_sem=recv_sem.at[step, n],
                device_id=device(offset),
                device_id_type=MESH,
            )
            copy.start()
            copies.append(copy)
        for copy in copies:
            copy.wait()
        for side in range(2):
            for k, p in enumerate(CROSSING[side]):
                field[p, 0 if side == 0 else nx + 1, PAD : PAD + ny, :] = x_recv[step, side, k]

        def unpack(x, carry):
            for side in range(2):
                row = PAD - 1 if side == 0 else PAD + ny
                for k, p in enumerate(CROSSING[2 + side]):
                    field[p, x + 1, row : row + 1, :] = y_recv[step, side, k, pl.ds(x, 1), :]
            return carry

        lax.fori_loop(0, nx, unpack, 0)
        for c, (dx, dy) in enumerate(CORNERS):
            low = 0 if dy == 1 else PAD + ny
            field[7 + c, 0 if dx == 1 else nx + 1, low : low + PAD, :] = c_recv[step, c]

    starts = range(0, ny, BS)

    def begin(x, carry):
        for start in starts:
            values = [pop_ref[p, x, start : start + BS, :].astype(jnp.float32) for p in range(POPS)]
            put(first, x, start, collide(values, rate_ref[start : start + BS, :]))
        return carry

    def middle(x, carry):
        for start in starts:
            values = gather(first, x, start)
            put(second, x, start, collide(values, rate_ref[start : start + BS, :]))
        return carry

    def finish(x, carry):
        for start in starts:
            values = gather(second, x, start)
            for p in range(POPS):
                out_ref[p, x, start : start + BS, :] = values[p].astype(jnp.bfloat16)
        return carry

    lax.fori_loop(0, nx, begin, 0)
    exchange(0, first)
    lax.fori_loop(0, nx, middle, 0)
    exchange(1, second)
    lax.fori_loop(0, nx, finish, 0)


def run_steps(populations, rates):
    _, nx, ny, nz = populations.shape
    field = pltpu.VMEM((POPS, nx + 2, ny + 2 * PAD, nz), jnp.float32)
    x_face = pltpu.VMEM((2, 2, 5, ny, nz), jnp.float32)
    y_face = pltpu.VMEM((2, 2, 5, nx, nz), jnp.float32)
    corner = pltpu.VMEM((2, 4, PAD, nz), jnp.float32)
    return pl.pallas_call(
        functools.partial(steps_kernel, nx, ny),
        out_shape=jax.ShapeDtypeStruct(populations.shape, jnp.bfloat16),
        in_specs=[pl.BlockSpec(memory_space=pltpu.VMEM)] * 2,
        out_specs=pl.BlockSpec(memory_space=pltpu.VMEM),
        scratch_shapes=[
            field,
            field,
            x_face,
            x_face,
            y_face,
            y_face,
            corner,
            corner,
            pltpu.SemaphoreType.DMA((2, len(NEIGHBOURS))),
            pltpu.SemaphoreType.DMA((2, len(NEIGHBOURS))),
        ],
        compiler_params=pltpu.CompilerParams(
            collective_id=0, has_side_effects=True, vmem_limit_bytes=48 * 2**20
        ),
        name="steps",
    )(populations, rates)


ROWS = 32
CHUNK = 4


def layout_kernel(nx, ny, nz, state_ref, select_ref, pool_ref, fine, packed):
    eighths = ny // 8
    across = nz // BS
    fine[...] = jnp.zeros_like(fine)

    def part(c, carry):
        for inner in range(CHUNK):
            x = c * CHUNK + inner
            for p in range(POPS):
                fine[p * ny : (p + 1) * ny, :] = state_ref[p, x].astype(jnp.float32)
            for e in range(eighths):
                row = (inner * eighths + e) * ROWS
                for j in range(8):
                    rows = fine[pl.ds(e * 8 + j, ROWS, stride=ny), :]
                    packed[row : row + ROWS, j * nz : (j + 1) * nz] = rows.astype(jnp.bfloat16)
        result = jnp.dot(packed[...], select_ref[...], preferred_element_type=jnp.float32)
        result = result.astype(jnp.bfloat16)
        for inner in range(CHUNK):
            for e in range(eighths):
                row = (inner * eighths + e) * ROWS
                lanes = pl.ds(pl.multiple_of((c * CHUNK * 2 + inner * 2 + e % 2) * 128, 128), 128)
                for k in range(across):
                    pool_ref[e // 2 * across + k, :, lanes] = result[
                        row : row + POPS, k * 128 : (k + 1) * 128
                    ]
        return carry

    lax.fori_loop(0, nx // CHUNK, part, 0)


def lay_out(state):
    _, nx, ny, nz = state.shape
    across = nz // BS
    select = np.zeros((8 * nz, across * 128), np.float32)
    for j in range(8):
        for z in range(nz):
            select[j * nz + z, z // BS * 128 + j * BS + z % BS] = 1.0
    blocks = ny // BS * across
    return pl.pallas_call(
        functools.partial(layout_kernel, nx, ny, nz),
        out_shape=jax.ShapeDtypeStruct((blocks, POPS, BS**3), jnp.bfloat16),
        in_specs=[pl.BlockSpec(memory_space=pltpu.VMEM)] * 2,
        out_specs=pl.BlockSpec(memory_space=pltpu.VMEM),
        scratch_shapes=[
            pltpu.VMEM((ROWS * ny, nz), jnp.float32),
            pltpu.VMEM((CHUNK * (ny // 8) * ROWS, 8 * nz), jnp.bfloat16),
        ],
        compiler_params=pltpu.CompilerParams(vmem_limit_bytes=48 * 2**20),
        name="layout",
    )(state, jnp.asarray(select, jnp.bfloat16))


def fill_kernel(source_ref, pool_ref, arrival_ref, empty_ref, out_ref, sem):
    blocks = pool_ref.shape[0]
    arrivals = arrival_ref.shape[0]

    def begin(slot, carry):
        source = source_ref[slot]

        @pl.when(source < blocks)
        def _():
            index = jnp.minimum(source, blocks - 1)
            pltpu.make_async_copy(pool_ref.at[index], out_ref.at[slot], sem.at[slot]).start()

        @pl.when((source >= blocks) & (source < blocks + arrivals))
        def _():
            index = jnp.clip(source - blocks, 0, arrivals - 1)
            pltpu.make_async_copy(arrival_ref.at[index], out_ref.at[slot], sem.at[slot]).start()

        @pl.when(source >= blocks + arrivals)
        def _():
            pltpu.make_async_copy(empty_ref, out_ref.at[slot], sem.at[slot]).start()

        return carry

    def end(slot, carry):
        pltpu.make_async_copy(empty_ref, out_ref.at[slot], sem.at[slot]).wait()
        return carry

    lax.fori_loop(0, CAP, begin, 0)
    lax.fori_loop(0, CAP, end, 0)


def fill(source, pool, arrivals):
    empty = jnp.zeros(pool.shape[1:], jnp.bfloat16)
    return pl.pallas_call(
        fill_kernel,
        out_shape=jax.ShapeDtypeStruct((CAP,) + pool.shape[1:], jnp.bfloat16),
        in_specs=[pl.BlockSpec(memory_space=pltpu.SMEM)] + [pl.BlockSpec(memory_space=pl.ANY)] * 3,
        out_specs=pl.BlockSpec(memory_space=pl.ANY),
        scratch_shapes=[pltpu.SemaphoreType.DMA((CAP,))],
        name="fill",
    )(source, pool, arrivals, empty)


def transfer_matrices():
    parent = np.arange(BS) // 2
    step = np.where(np.arange(BS) % 2 == 0, -1, 1)
    neighbour = np.clip(parent + step, 0, HALF - 1)
    inject = (parent[:, None] == np.arange(HALF)[None, :]).astype(np.float32)
    linear = 0.75 * inject + 0.25 * (neighbour[:, None] == np.arange(HALF)[None, :])

    def cube(matrix):
        return np.kron(np.kron(matrix, matrix), matrix)

    merge = cube(inject) * 0.125
    spread = np.concatenate([cube(inject).T, cube(linear).T], axis=0)
    return merge, spread


def body(populations, levels, refine_flags, new_owner):
    slab_count = lax.axis_size("gx")
    column_count = lax.axis_size("yz")
    slab = lax.axis_index("gx")
    column = lax.axis_index("yz")
    me = slab * column_count + column
    devices = slab_count * column_count
    _, nx, ny, nz = populations.shape
    across = nz // BS
    rows = ny // BS
    local = rows * across
    base = me * local
    block_total = new_owner.shape[0]

    local_levels = lax.dynamic_slice(levels, (base,), (local,)).reshape(rows, across)
    block_rates = 1.0 / (0.5 + jnp.power(0.5, local_levels.astype(jnp.float32)))
    rates = jnp.repeat(jnp.repeat(block_rates, BS, 0), BS, 1)

    ids = jnp.arange(block_total, dtype=jnp.int32)
    owned = new_owner == me
    before = owned[None, :] & (ids[None, :] < ids[:, None])
    rank = jnp.sum(before.astype(jnp.int32), axis=1)
    slots = jnp.arange(CAP, dtype=jnp.int32)
    hit = owned[None, :] & (rank[None, :] == slots[:, None])
    slot_id = jnp.sum(jnp.where(hit, ids[None, :], 0), axis=1)
    slot_kind = jnp.sum(jnp.where(hit, refine_flags[None, :], 0), axis=1)
    slot_used = jnp.any(hit, axis=1)
    flagged = slot_kind != 0
    slot_rank = jnp.sum(
        (flagged[None, :] & (slots[None, :] < slots[:, None])).astype(jnp.int32), axis=1
    )
    order = jnp.arange(2 * MIG, dtype=jnp.int32)
    match = flagged[None, :] & (slot_rank[None, :] == order[:, None])
    arrival_id = jnp.sum(jnp.where(match, slot_id[None, :], 0), axis=1)
    arrival_kind = jnp.sum(jnp.where(match, slot_kind[None, :], 0), axis=1)
    source = jnp.where(
        slot_used,
        jnp.where(flagged, local + slot_rank, slot_id % local),
        local + 2 * MIG,
    )

    local_flags = lax.dynamic_slice(refine_flags, (base,), (local,))
    local_owner = lax.dynamic_slice(new_owner, (base,), (local,))
    leaving = (local_flags != 0)[None, :] & (
        local_owner[None, :] == jnp.arange(devices, dtype=jnp.int32)[:, None]
    )
    leaving_block = jnp.sum(
        jnp.where(leaving, jnp.arange(local, dtype=jnp.int32)[None, :], 0), axis=1
    )

    state = run_steps(populations, rates)
    pool = lay_out(state)
    merge, spread = transfer_matrices()
    coarse = jnp.einsum(
        "bpf,fc->bpc",
        pool,
        jnp.asarray(merge, jnp.bfloat16),
        preferred_element_type=jnp.float32,
    ).astype(jnp.bfloat16)
    outgoing = jnp.take(coarse, leaving_block, axis=0)
    incoming = lax.all_to_all(outgoing, ("gx", "yz"), split_axis=0, concat_axis=0, tiled=True)
    arrived = jnp.take(incoming, arrival_id // local, axis=0)
    zero = jnp.zeros((), jnp.bfloat16)
    kinds = arrival_kind[:, None, None]
    both = jnp.concatenate(
        [jnp.where(kinds == 1, arrived, zero), jnp.where(kinds == 2, arrived, zero)], axis=2
    )
    refined = jnp.einsum(
        "bpc,cf->bpf",
        both,
        jnp.asarray(spread, jnp.bfloat16),
        preferred_element_type=jnp.float32,
    ).astype(jnp.bfloat16)
    return fill(source, pool, refined)


def solution(mesh):
    placed = (P(None, "gx", "yz", None), P(), P(), P())
    return jax.shard_map(
        body, mesh=mesh, in_specs=placed, out_specs=P(("gx", "yz"), None, None), check_vma=False
    )
```

profile of v0, /device:TPU:1, one launch (start us, length us, event | category | flops | bytes accessed | tf_op | source)
XLA Modules:
  0.0 228.8 jit_solution(9326061321860039812)
XLA Ops:
  0.0 0.8 dynamic-slice_compare_fusion
  0.8 0.8 dynamic_slice.11
  1.5 0.1 select_reduce_fusion.2
  1.6 0.8 add_divide_fusion
  2.4 0.1 div.27
  2.5 0.1 copy.12
  2.6 0.1 broadcast_in_dim.124
  2.6 0.1 reshape.114
  2.7 0.1 copy.13.rate_ref
  2.8 0.0 copy-start
  2.8 1.7 copy-done
  4.5 0.0 copy-start.1
  4.5 21.5 %steps.1.state_ref = bf16[19,16,32,128]{3,2,1,0:T(8,128)(2,1)S(1)} custom-call(bf16[19,16,32,128]{3,2,1,0:T(8,128)(2,1)S(1)} %copy-done, f32[32,128]{1,0:T(8,128)S(1)} %copy.13.rate_ref), custom_call_target="tpu_custom_call" | custom-call | tf_op jit(solution)/shard_map/steps/pallas_call | solution.py:248
  26.1 0.0 copy-done.1
  26.1 0.0 copy-start.4
  26.1 12.4 %layout.1.pool_ref = bf16[16,19,4096]{2,1,0:T(8,128)(2,1)} custom-call(bf16[19,16,32,128]{3,2,1,0:T(8,128)(2,1)S(1)} %steps.1.state_ref, bf16[1024,1024]{1,0:T(8,128)(2,1)S(1)} %copy-done.1), custom_call_target="tpu_custom_call" | custom-call | tf_op jit(solution)/shard_map/layout/pallas_call | solution.py:314
  38.5 0.0 copy-done.4
  38.5 3.7 %convolution_convert_fusion.1 = bf16[16,19,512]{2,1,0:T(8,128)(2,1)S(1)} fusion(bf16[16,19,4096]{2,1,0:T(8,128)(2,1)} %layout.1.pool_ref, bf16[4096,512,1]{1,0,2:T(8,128)(2,1)S(1)} %copy-done.4), kind=kOutput, calls=%fused_computation.3 | convolution fusion | flops 1275224064 | bytes 6995968 | tf_op jit(solution)/shard_map/bpf,fc->bpc/dot_general | solution.py:439
  42.2 0.0 copy-start.2
  42.2 0.0 copy-start.3
  42.2 0.6 gather_fusion
  42.8 1.0 broadcast_select_fusion
  43.8 3.2 %all-to-all-start = ((bf16[32,19,512]{2,1,0:T(8,128)(2,1)}), bf16[32,19,512]{2,1,0:T(8,128)(2,1)S(1)}, u32[]{:S(2)}, u32[]{:S(2)}) async-start(bf16[32,19,512]{2,1,0:T(8,128)(2,1)} %broadcast_select_fusion), calls=%async_computation | async-start | bytes 1572864 | tf_op jit(solution)/shard_map/all_to_all | solution.py:446
  47.1 0.0 copy-done.2
  47.1 0.1 convert_reduce_fusion
  47.2 0.0 copy-done.3
  47.2 0.1 select_reduce_fusion.1
  47.4 0.1 convert_reduce_fusion.1
  47.5 0.1 select_reduce_fusion.3
  47.6 0.1 fusion.5
  47.8 0.6 fusion.13.source_ref
  48.4 19.5 %all-to-all-done = bf16[32,19,512]{2,1,0:T(8,128)(2,1)S(1)} async-done(((bf16[32,19,512]{2,1,0:T(8,128)(2,1)}), bf16[32,19,512]{2,1,0:T(8,128)(2,1)S(1)}, u32[]{:S(2)}, u32[]{:S(2)}) %all-to-all-start) | async-done | bytes 622624 | tf_op jit(solution)/shard_map/all_to_all | solution.py:446
  67.9 0.6 gather_fusion.1
  68.5 0.1 broadcast_select_fusion.3
  68.6 8.2 %convolution_convert_fusion.arrival_ref = bf16[16,19,4096]{2,1,0:T(8,128)(2,1)} fusion(bf16[1024,4096,1]{1,0,2:T(8,128)(2,1)} %constant.94, bf16[16,19,512]{2,1,0:T(8,128)(2,1)S(1)} %get-tuple-element.10, bf16[16,19,512]{2,1,0:T(8,128)(2,1)S(1)} %get-tuple-element.9), kind=kOutput, calls=%fused_computation.2 | convolution fusion | flops 2552627200 | bytes 11501568 | tf_op jit(solution)/shard_map/bpc,cf->bpf/dot_general | solution.py:453
  76.8 0.7 broadcast_in_dim.138.empty_ref
  77.5 144.9 %fill.1 = bf16[24,19,4096]{2,1,0:T(8,128)(2,1)} custom-call(s32[24]{0:T(128)} %fusion.13.source_ref, bf16[16,19,4096]{2,1,0:T(8,128)(2,1)} %layout.1.pool_ref, bf16[16,19,4096]{2,1,0:T(8,128)(2,1)} %convolution_convert_fusion.arrival_ref, bf16[19,4096]{1,0:T(8,128)(2,1)} %broadcast_in_dim.138.empty_ref), custom_call_target="tpu_custom_call" | custom-call | tf_op jit(solution)/shard_map/fill/pallas_call | solution.py:361
  222.4 6.3 %copy.14 = bf16[24,19,4096]{2,0,1:T(8,128)(2,1)} copy(bf16[24,19,4096]{2,1,0:T(8,128)(2,1)} %fill.1) | data formatting | bytes 7471104 | tf_op jit(solution)/shard_map/fill/pallas_call | solution.py:361
  (9 shorter events, 0.1 us)
Async XLA Ops:
  2.8 1.7 copy-start
  4.5 21.5 %copy-start.1 = (bf16[1024,1024]{1,0:T(8,128)(2,1)S(1)}, bf16[1024,1024]{1,0:T(8,128)(2,1)}, u32[]{:S(2)}) copy-start(bf16[1024,1024]{1,0:T(8,128)(2,1)} %constant.90.clone.select_ref) | copy-start | bytes 6291460
  26.1 12.4 %copy-start.4 = (bf16[4096,512,1]{1,0,2:T(8,128)(2,1)S(1)}, bf16[4096,512,1]{1,0,2:T(8,128)(2,1)}, u32[]{:S(2)}) copy-start(bf16[4096,512,1]{1,0,2:T(8,128)(2,1)} %constant.93) | copy-start | bytes 12582916
  42.2 4.9 %copy-start.2 = (s32[512]{0:T(512)S(1)}, s32[512]{0:T(512)}, u32[]{:S(2)}) copy-start(s32[512]{0:T(512)} %param.10) | copy-start | bytes 6148
  42.2 5.1 %copy-start.3 = (s32[512]{0:T(512)S(1)}, s32[512]{0:T(512)}, u32[]{:S(2)}) copy-start(s32[512]{0:T(512)} %param.9) | copy-start | bytes 6148
  43.8 24.1 %all-to-all-start = ((bf16[32,19,512]{2,1,0:T(8,128)(2,1)}), bf16[32,19,512]{2,1,0:T(8,128)(2,1)S(1)}, u32[]{:S(2)}, u32[]{:S(2)}) async-start(bf16[32,19,512]{2,1,0:T(8,128)(2,1)} %broadcast_select_fusion), calls=%async_computation | async-start | bytes 1572864 | tf_op jit(solution)/shard_map/all_to_all | solution.py:446
where the time goes:
time: 229 us
  Pallas kernels  179 us (78%)
  waiting for transfers between devices  19.5 us (9%)
  matrix products  11.9 us (5%)
  local copies, waits for them, and re-layouts  11.1 us (5%)
  other arithmetic  4.07 us (2%)
  starting transfers between devices  3.24 us (1%)
    pallas_call x1, Pallas kernels, fill(): pl.pallas_call(fill_kernel, out_shape=jax.ShapeDtypeStruct((CAP,) + pool....  145 us
    pallas_call x1, Pallas kernels, run_steps(): pl.pallas_call(functools.partial(steps_kernel, nx, ny), out_shape=jax.Sha...  21.5 us
    all_to_all x1, waiting for transfers between devices, body(): lax.all_to_all(outgoing, ('gx', 'yz'), split_axis=0, concat_axis=0, tiled...  19.5 us
    pallas_call x1, Pallas kernels, lay_out(): pl.pallas_call(functools.partial(layout_kernel, nx, ny, nz), out_shape=ja...  12.4 us
    dot_general x1, matrix products, body(): jnp.einsum('bpc,cf->bpf', both, jnp.asarray(spread, jnp.bfloat16), prefer...  8.18 us
    pallas_call x1, local copies, waits for them, and re-layouts, fill(): pl.pallas_call(fill_kernel, out_shape=jax.ShapeDtypeStruct((CAP,) + pool....  6.34 us
  transfers between devices with their start and end apart: 1, of which 1 were waited for; matrix products, arithmetic and copies ran while one was open for 1% of the time, Pallas kernels for 0%

commit v1 on v0

--- a/solution.py
+++ b/solution.py
@@ -325,47 +325,60 @@
     )(state, jnp.asarray(select, jnp.bfloat16))
 
 
-def fill_kernel(source_ref, pool_ref, arrival_ref, empty_ref, out_ref, sem):
+def fill_kernel(source_ref, pool_ref, arrival_ref, out_ref, held):
     blocks = pool_ref.shape[0]
     arrivals = arrival_ref.shape[0]
 
-    def begin(slot, carry):
+    def place(slot, carry):
         source = source_ref[slot]
+        rows = pl.ds(slot, POPS, stride=CAP)
 
         @pl.when(source < blocks)
         def _():
-            index = jnp.minimum(source, blocks - 1)
-            pltpu.make_async_copy(pool_ref.at[index], out_ref.at[slot], sem.at[slot]).start()
+            value = pool_ref[jnp.minimum(source, blocks - 1)].astype(jnp.float32)
+            for k in range(LANES):
+                held[k, rows, :] = value[:, k * 128 : (k + 1) * 128]
 
         @pl.when((source >= blocks) & (source < blocks + arrivals))
         def _():
             index = jnp.clip(source - blocks, 0, arrivals - 1)
-            pltpu.make_async_copy(arrival_ref.at[index], out_ref.at[slot], sem.at[slot]).start()
+            value = arrival_ref[index].astype(jnp.float32)
+            for k in range(LANES):
+                held[k, rows, :] = value[:, k * 128 : (k + 1) * 128]
 
         @pl.when(source >= blocks + arrivals)
         def _():
-            pltpu.make_async_copy(empty_ref, out_ref.at[slot], sem.at[slot]).start()
-
-        return carry
-
-    def end(slot, carry):
-        pltpu.make_async_copy(empty_ref, out_ref.at[slot], sem.at[slot]).wait()
-        return carry
-
-    lax.fori_loop(0, CAP, begin, 0)
-    lax.fori_loop(0, CAP, end, 0)
+            for k in range(LANES):
+                held[k, rows, :] = jnp.zeros((POPS, 128), jnp.float32)
+
+        return carry
+
+    lax.fori_loop(0, CAP, place, 0)
+
+    def emit(p, carry):
+        rows = pl.ds(pl.multiple_of(p * CAP, 8), CAP)
+        for k in range(LANES):
+            out_ref[p, :, k * 128 : (k + 1) * 128] = held[k, rows, :].astype(jnp.bfloat16)
+        return carry
+
+    lax.fori_loop(0, POPS, emit, 0)
+
+
+LANES = BS**3 // 128
 
 
 def fill(source, pool, arrivals):
-    empty = jnp.zeros(pool.shape[1:], jnp.bfloat16)
-    return pl.pallas_call(
+    slotted = pl.pallas_call(
         fill_kernel,
-        out_shape=jax.ShapeDtypeStruct((CAP,) + pool.shape[1:], jnp.bfloat16),
-        in_specs=[pl.BlockSpec(memory_space=pltpu.SMEM)] + [pl.BlockSpec(memory_space=pl.ANY)] * 3,
-        out_specs=pl.BlockSpec(memory_space=pl.ANY),
-        scratch_shapes=[pltpu.SemaphoreType.DMA((CAP,))],
+        out_shape=jax.ShapeDtypeStruct((POPS, CAP, BS**3), jnp.bfloat16),
+        in_specs=[pl.BlockSpec(memory_space=pltpu.SMEM)]
+        + [pl.BlockSpec(memory_space=pltpu.VMEM)] * 2,
+        out_specs=pl.BlockSpec(memory_space=pltpu.VMEM),
+        scratch_shapes=[pltpu.VMEM((LANES, POPS * CAP, 128), jnp.float32)],
+        compiler_params=pltpu.CompilerParams(vmem_limit_bytes=48 * 2**20),
         name="fill",
-    )(source, pool, arrivals, empty)
+    )(source, pool, arrivals)
+    return jnp.transpose(slotted, (1, 0, 2))
 
 
 def transfer_matrices():

time: 229 us -> 84 us (0.37)
  Pallas kernels: 179 us -> 40.5 us
  local copies, waits for them, and re-layouts: 11.1 us -> 4.07 us
    pallas_call x1, Pallas kernels: 145 us -> 6.61 us  [fill(): pl.pallas_call(fill_kernel, out_shape=jax.ShapeDtypeStruct((POPS, CAP, BS...]
    pallas_call x1 -> x0, local copies, waits for them, and re-layouts: 6.34 us -> none  [fill(): pl.pallas_call(fill_kernel, out_shape=jax.ShapeDtypeStruct((CAP,) + pool....]
where the time goes in v1:
time: 84 us; the launch traced here: 83.6 us
  Pallas kernels  40.5 us (48%)
  waiting for transfers between devices  20.1 us (24%)
  matrix products  12 us (14%)
  local copies, waits for them, and re-layouts  4.07 us (5%)
  other arithmetic  3.5 us (4%)
  starting transfers between devices  3.24 us (4%)
    pallas_call x1, Pallas kernels, run_steps(): pl.pallas_call(functools.partial(steps_kernel, nx, ny), out_shape=jax.Sha...  21.5 us
    all_to_all x1, waiting for transfers between devices, body(): lax.all_to_all(outgoing, ('gx', 'yz'), split_axis=0, concat_axis=0, tiled...  20.1 us
    pallas_call x1, Pallas kernels, lay_out(): pl.pallas_call(functools.partial(layout_kernel, nx, ny, nz), out_shape=ja...  12.4 us
    dot_general x1, matrix products, body(): jnp.einsum('bpc,cf->bpf', both, jnp.asarray(spread, jnp.bfloat16), prefer...  8.34 us
    pallas_call x1, Pallas kernels, fill(): pl.pallas_call(fill_kernel, out_shape=jax.ShapeDtypeStruct((POPS, CAP, BS...  6.61 us
    dot_general x1, matrix products, body(): jnp.einsum('bpf,fc->bpc', pool, jnp.asarray(merge, jnp.bfloat16), preferr...  3.68 us
    all_to_all x1, starting transfers between devices, body(): lax.all_to_all(outgoing, ('gx', 'yz'), split_axis=0, concat_axis=0, tiled...  3.24 us
    unnamed x12, local copies, waits for them, and re-layouts  1.76 us
  transfers between devices with their start and end apart: 1, of which 1 were waited for; matrix products, arithmetic and copies ran while one was open for 1% of the time, Pallas kernels for 0%

profile of v1, /device:TPU:1, one launch (start us, length us, event | category | flops | bytes accessed | tf_op | source)
XLA Modules:
  0.0 83.6 jit_solution(13851749283580658992)
XLA Ops:
  0.0 0.8 dynamic-slice_compare_fusion
  0.8 0.8 dynamic_slice.11
  1.5 0.1 select_reduce_fusion.2
  1.6 0.8 add_divide_fusion
  2.4 0.1 div.27
  2.5 0.1 copy.10
  2.6 0.1 broadcast_in_dim.121
  2.6 0.1 reshape.114
  2.7 0.1 copy.11.rate_ref
  2.8 0.0 copy-start.1
  2.8 1.7 %copy-done.1 = bf16[19,16,32,128]{3,2,1,0:T(8,128)(2,1)S(1)} copy-done((bf16[19,16,32,128]{3,2,1,0:T(8,128)(2,1)S(1)}, bf16[19,16,32,128]{3,2,1,0:T(8,128)(2,1)}, u32[]{:S(2)}) %copy-start.1) | copy-done | bytes 2490392
  4.5 0.0 copy-start.2
  4.5 21.5 %steps.1.state_ref = bf16[19,16,32,128]{3,2,1,0:T(8,128)(2,1)S(1)} custom-call(bf16[19,16,32,128]{3,2,1,0:T(8,128)(2,1)S(1)} %copy-done.1, f32[32,128]{1,0:T(8,128)S(1)} %copy.11.rate_ref), custom_call_target="tpu_custom_call" | custom-call | tf_op jit(solution)/shard_map/steps/pallas_call | solution.py:248
  26.1 0.0 copy-done.2
  26.1 0.0 copy-start.5
  26.1 12.4 %layout.1.pool_ref = bf16[16,19,4096]{2,1,0:T(8,128)(2,1)} custom-call(bf16[19,16,32,128]{3,2,1,0:T(8,128)(2,1)S(1)} %steps.1.state_ref, bf16[1024,1024]{1,0:T(8,128)(2,1)S(1)} %copy-done.2), custom_call_target="tpu_custom_call" | custom-call | tf_op jit(solution)/shard_map/layout/pallas_call | solution.py:314
  38.5 0.0 copy-done.5
  38.5 3.7 %convolution_convert_fusion.1 = bf16[16,19,512]{2,1,0:T(8,128)(2,1)S(1)} fusion(bf16[16,19,4096]{2,1,0:T(8,128)(2,1)} %layout.1.pool_ref, bf16[4096,512,1]{1,0,2:T(8,128)(2,1)S(1)} %copy-done.5), kind=kOutput, calls=%fused_computation.3 | convolution fusion | flops 1275224064 | bytes 6995968 | tf_op jit(solution)/shard_map/bpf,fc->bpc/dot_general | solution.py:452
  42.2 0.0 copy-start.3
  42.2 0.0 copy-start.4
  42.2 0.6 gather_fusion
  42.8 1.0 %broadcast_select_fusion = bf16[32,19,512]{2,1,0:T(8,128)(2,1)} fusion(bf16[32,19,512]{2,1,0:T(8,128)(2,1)S(1)} %gather_fusion, pred[32]{0:T(512)(128)(4,1)S(1)} %compare_and_fusion), kind=kLoop, calls=%fused_computation.10 | loop fusion | flops 311296 | bytes 1245216 | tf_op jit(solution)/shard_map/jit(_take)/select_n | solution.py:458
  43.8 3.2 %all-to-all-start = ((bf16[32,19,512]{2,1,0:T(8,128)(2,1)}), bf16[32,19,512]{2,1,0:T(8,128)(2,1)S(1)}, u32[]{:S(2)}, u32[]{:S(2)}) async-start(bf16[32,19,512]{2,1,0:T(8,128)(2,1)} %broadcast_select_fusion), calls=%async_computation | async-start | bytes 1572864 | tf_op jit(solution)/shard_map/all_to_all | solution.py:459
  47.1 0.0 copy-done.3
  47.1 0.1 convert_reduce_fusion
  47.2 0.0 copy-done.4
  47.2 0.1 select_reduce_fusion.1
  47.4 0.1 convert_reduce_fusion.1
  47.5 0.1 select_reduce_fusion.3
  47.6 0.1 fusion.5
  47.8 20.1 %all-to-all-done = bf16[32,19,512]{2,1,0:T(8,128)(2,1)S(1)} async-done(((bf16[32,19,512]{2,1,0:T(8,128)(2,1)}), bf16[32,19,512]{2,1,0:T(8,128)(2,1)S(1)}, u32[]{:S(2)}, u32[]{:S(2)}) %all-to-all-start) | async-done | bytes 622624 | tf_op jit(solution)/shard_map/all_to_all | solution.py:459
  67.9 0.6 gather_fusion.1
  68.5 0.1 broadcast_select_fusion.3
  68.6 0.0 copy-start
  68.6 8.3 %convolution_convert_fusion.arrival_ref = bf16[16,19,4096]{2,1,0:T(8,128)(2,1)} fusion(bf16[1024,4096,1]{1,0,2:T(8,128)(2,1)} %constant.93, bf16[16,19,512]{2,1,0:T(8,128)(2,1)S(1)} %get-tuple-element.10, bf16[16,19,512]{2,1,0:T(8,128)(2,1)S(1)} %get-tuple-element.9), kind=kOutput, calls=%fused_computation.2 | convolution fusion | flops 2552627200 | bytes 11501568 | tf_op jit(solution)/shard_map/bpc,cf->bpf/dot_general | solution.py:466
  77.0 0.0 copy-done
  77.0 6.6 %fill.1 = bf16[19,24,4096]{2,1,0:T(8,128)(2,1)} custom-call(s32[24]{0:T(128)S(1)} %fusion.13.source_ref, bf16[16,19,4096]{2,1,0:T(8,128)(2,1)S(1)} %copy-done, bf16[16,19,4096]{2,1,0:T(8,128)(2,1)} %convolution_convert_fusion.arrival_ref), custom_call_target="tpu_custom_call" | custom-call | tf_op jit(solution)/shard_map/fill/pallas_call | solution.py:371
  (10 shorter events, 0.1 us)
Async XLA Ops:
  2.8 1.7 %copy-start.1 = (bf16[19,16,32,128]{3,2,1,0:T(8,128)(2,1)S(1)}, bf16[19,16,32,128]{3,2,1,0:T(8,128)(2,1)}, u32[]{:S(2)}) copy-start(bf16[19,16,32,128]{3,2,1,0:T(8,128)(2,1)} %pop_ref.1) | copy-start | bytes 7471108
  4.5 21.5 %copy-start.2 = (bf16[1024,1024]{1,0:T(8,128)(2,1)S(1)}, bf16[1024,1024]{1,0:T(8,128)(2,1)}, u32[]{:S(2)}) copy-start(bf16[1024,1024]{1,0:T(8,128)(2,1)} %constant.89.clone.select_ref) | copy-start | bytes 6291460
  26.1 12.4 %copy-start.5 = (bf16[4096,512,1]{1,0,2:T(8,128)(2,1)S(1)}, bf16[4096,512,1]{1,0,2:T(8,128)(2,1)}, u32[]{:S(2)}) copy-start(bf16[4096,512,1]{1,0,2:T(8,128)(2,1)} %constant.92) | copy-start | bytes 12582916
  42.2 4.9 %copy-start.3 = (s32[512]{0:T(512)S(1)}, s32[512]{0:T(512)}, u32[]{:S(2)}) copy-start(s32[512]{0:T(512)} %param.10) | copy-start | bytes 6148
  42.2 5.1 %copy-start.4 = (s32[512]{0:T(512)S(1)}, s32[512]{0:T(512)}, u32[]{:S(2)}) copy-start(s32[512]{0:T(512)} %param.9) | copy-start | bytes 6148
  43.8 24.1 %all-to-all-start = ((bf16[32,19,512]{2,1,0:T(8,128)(2,1)}), bf16[32,19,512]{2,1,0:T(8,128)(2,1)S(1)}, u32[]{:S(2)}, u32[]{:S(2)}) async-start(bf16[32,19,512]{2,1,0:T(8,128)(2,1)} %broadcast_select_fusion), calls=%async_computation | async-start | bytes 1572864 | tf_op jit(solution)/shard_map/all_to_all | solution.py:459
  68.6 8.4 %copy-start = (bf16[16,19,4096]{2,1,0:T(8,128)(2,1)S(1)}, bf16[16,19,4096]{2,1,0:T(8,128)(2,1)}, u32[]{:S(2)}) copy-start(bf16[16,19,4096]{2,1,0:T(8,128)(2,1)} %layout.1.pool_ref) | copy-start | bytes 7471108

commit v2 on v1

--- a/solution.py
+++ b/solution.py
@@ -320,14 +320,120 @@
             pltpu.VMEM((ROWS * ny, nz), jnp.float32),
             pltpu.VMEM((CHUNK * (ny // 8) * ROWS, 8 * nz), jnp.bfloat16),
         ],
-        compiler_params=pltpu.CompilerParams(vmem_limit_bytes=48 * 2**20),
+        compiler_params=pltpu.CompilerParams(vmem_limit_bytes=32 * 2**20),
+        cost_estimate=pl.CostEstimate(
+            flops=2 * state.size * across * 128, bytes_accessed=8 * state.size, transcendentals=0
+        ),
         name="layout",
     )(state, jnp.asarray(select, jnp.bfloat16))
 
 
-def fill_kernel(source_ref, pool_ref, arrival_ref, out_ref, held):
+LANES = BS**3 // 128
+QUADS = HALF // 2
+
+
+def merge_kernel(nx, ny, leaving_ref, state_ref, shrink_ref, select_ref, out_ref, fine, packed, held):
+    nz = state_ref.shape[3]
+    rows = ny // BS
+    across = nz // BS
+    groups = nx // 4
+    fine[...] = jnp.zeros_like(fine)
+    for p in range(POPS):
+        planes = [
+            jnp.concatenate([state_ref[p, g * 4 + i] for i in range(4)], axis=1)
+            for g in range(groups)
+        ]
+        fine[p * groups * ny : (p + 1) * groups * ny, :] = jnp.dot(
+            jnp.concatenate(planes, axis=0), shrink_ref[...], preferred_element_type=jnp.float32
+        )
+    for g in range(groups):
+        for r in range(rows):
+            row = (g * rows + r) * ROWS
+            for j in range(HALF):
+                start = g * ny + r * BS + 2 * j
+                value = (
+                    fine[pl.ds(start, ROWS, stride=groups * ny), :]
+                    + fine[pl.ds(start + 1, ROWS, stride=groups * ny), :]
+                )
+                packed[row : row + ROWS, j * 128 : (j + 1) * 128] = value.astype(jnp.bfloat16)
+    result = jnp.dot(packed[...], select_ref[...], preferred_element_type=jnp.float32)
+    result = result.astype(jnp.bfloat16)
+    for g in range(groups):
+        for r in range(rows):
+            row = (g * rows + r) * ROWS
+            for k in range(across):
+                held[r * across + k, :, g * 128 : (g + 1) * 128] = result[
+                    row : row + POPS, k * 128 : (k + 1) * 128
+                ]
+
+    def give(target, carry):
+        out_ref[target] = held[leaving_ref[target]]
+        return carry
+
+    lax.fori_loop(0, out_ref.shape[0], give, 0)
+
+
+def merge(leaving, state):
+    _, nx, ny, nz = state.shape
+    across = nz // BS
+    shrink = np.zeros((4, nz, 2, across, HALF), np.float32)
+    for i in range(4):
+        for z in range(nz):
+            shrink[i, z, i // 2, z // BS, z % BS // 2] = 0.125
+    shrink = shrink.reshape(4 * nz, 2 * across * HALF)
+    select = np.zeros((HALF, 2, across, HALF, across, 2, HALF, HALF), np.float32)
+    for j in range(HALF):
+        for half in range(2):
+            for k in range(across):
+                for z in range(HALF):
+                    select[j, half, k, z, k, half, j, z] = 1.0
+    select = select.reshape(HALF * 2 * across * HALF, across * 128)
+    blocks = ny // BS * across
+    groups = nx // 4
+    return pl.pallas_call(
+        functools.partial(merge_kernel, nx, ny),
+        out_shape=jax.ShapeDtypeStruct((leaving.shape[0], POPS, HALF**3), jnp.bfloat16),
+        in_specs=[pl.BlockSpec(memory_space=pltpu.SMEM)]
+        + [pl.BlockSpec(memory_space=pltpu.VMEM)] * 3,
+        out_specs=pl.BlockSpec(memory_space=pltpu.VMEM),
+        scratch_shapes=[
+            pltpu.VMEM((ROWS * groups * ny, 128), jnp.float32),
+            pltpu.VMEM((groups * (ny // BS) * ROWS, HALF * 128), jnp.bfloat16),
+            pltpu.VMEM((blocks, POPS, HALF**3), jnp.bfloat16),
+        ],
+        compiler_params=pltpu.CompilerParams(vmem_limit_bytes=32 * 2**20),
+        name="merge",
+    )(leaving, state, jnp.asarray(shrink, jnp.bfloat16), jnp.asarray(select, jnp.bfloat16))
+
+
+def fill_kernel(
+    source_ref, origin_ref, kind_ref, pool_ref, incoming_ref, spread_ref, out_ref, held, packed, wide
+):
     blocks = pool_ref.shape[0]
-    arrivals = arrival_ref.shape[0]
+    arrivals = origin_ref.shape[0]
+    packed[...] = jnp.zeros_like(packed)
+
+    def load(a, carry):
+        kind = kind_ref[a]
+        value = incoming_ref[origin_ref[a]]
+        zero = jnp.zeros_like(value)
+        for half in range(2):
+            part = jnp.where(kind == half + 1, value, zero)
+            for q in range(QUADS):
+                packed[a * QUADS + q, 0:POPS, half * 128 : (half + 1) * 128] = part[
+                    :, q * 128 : (q + 1) * 128
+                ]
+        return carry
+
+    lax.fori_loop(0, arrivals, load, 0)
+
+    def expand(a, carry):
+        rows = packed[pl.ds(a * 4 * QUADS, 4 * QUADS)].reshape(4 * QUADS * ROWS, 256)
+        product = jnp.dot(rows, spread_ref[...], preferred_element_type=jnp.float32)
+        wide[pl.ds(a * 4 * QUADS, 4 * QUADS)] = product.reshape(4 * QUADS, ROWS, 4 * 128)
+        return carry
+
+    lax.fori_loop(0, arrivals // 4, expand, 0)
 
     def place(slot, carry):
         source = source_ref[slot]
@@ -342,9 +448,18 @@
         @pl.when((source >= blocks) & (source < blocks + arrivals))
         def _():
             index = jnp.clip(source - blocks, 0, arrivals - 1)
-            value = arrival_ref[index].astype(jnp.float32)
-            for k in range(LANES):
-                held[k, rows, :] = value[:, k * 128 : (k + 1) * 128]
+            linear = kind_ref[index] == 2
+            near = jnp.where(linear, 0.75, 1.0)
+            far = jnp.where(linear, 0.25, 0.0)
+            for part in range(2):
+                slabs = []
+                for h in range(HALF):
+                    lane = h % 2 * 256 + part * 128
+                    slabs.append(wide[index * QUADS + h // 2, 0:POPS, lane : lane + 128])
+                for x in range(BS):
+                    h = x // 2
+                    other = max(h - 1, 0) if x % 2 == 0 else min(h + 1, HALF - 1)
+                    held[x * 2 + part, rows, :] = near * slabs[h] + far * slabs[other]
 
         @pl.when(source >= blocks + arrivals)
         def _():
@@ -364,36 +479,31 @@
     lax.fori_loop(0, POPS, emit, 0)
 
 
-LANES = BS**3 // 128
-
-
-def fill(source, pool, arrivals):
-    slotted = pl.pallas_call(
-        fill_kernel,
-        out_shape=jax.ShapeDtypeStruct((POPS, CAP, BS**3), jnp.bfloat16),
-        in_specs=[pl.BlockSpec(memory_space=pltpu.SMEM)]
-        + [pl.BlockSpec(memory_space=pltpu.VMEM)] * 2,
-        out_specs=pl.BlockSpec(memory_space=pltpu.VMEM),
-        scratch_shapes=[pltpu.VMEM((LANES, POPS * CAP, 128), jnp.float32)],
-        compiler_params=pltpu.CompilerParams(vmem_limit_bytes=48 * 2**20),
-        name="fill",
-    )(source, pool, arrivals)
-    return jnp.transpose(slotted, (1, 0, 2))
-
-
-def transfer_matrices():
+def fill(source, origin, kinds, pool, incoming):
     parent = np.arange(BS) // 2
     step = np.where(np.arange(BS) % 2 == 0, -1, 1)
     neighbour = np.clip(parent + step, 0, HALF - 1)
     inject = (parent[:, None] == np.arange(HALF)[None, :]).astype(np.float32)
     linear = 0.75 * inject + 0.25 * (neighbour[:, None] == np.arange(HALF)[None, :])
-
-    def cube(matrix):
-        return np.kron(np.kron(matrix, matrix), matrix)
-
-    merge = cube(inject) * 0.125
-    spread = np.concatenate([cube(inject).T, cube(linear).T], axis=0)
-    return merge, spread
+    spread = np.concatenate(
+        [np.kron(np.eye(2), np.kron(matrix, matrix).T) for matrix in (inject, linear)], axis=0
+    )
+    count = origin.shape[0]
+    slotted = pl.pallas_call(
+        fill_kernel,
+        out_shape=jax.ShapeDtypeStruct((POPS, CAP, BS**3), jnp.bfloat16),
+        in_specs=[pl.BlockSpec(memory_space=pltpu.SMEM)] * 3
+        + [pl.BlockSpec(memory_space=pltpu.VMEM)] * 3,
+        out_specs=pl.BlockSpec(memory_space=pltpu.VMEM),
+        scratch_shapes=[
+            pltpu.VMEM((LANES, POPS * CAP, 128), jnp.float32),
+            pltpu.VMEM((count * QUADS, ROWS, 256), jnp.bfloat16),
+            pltpu.VMEM((count * QUADS, ROWS, 512), jnp.float32),
+        ],
+        compiler_params=pltpu.CompilerParams(vmem_limit_bytes=48 * 2**20),
+        name="fill",
+    )(source, origin, kinds, pool, incoming, jnp.asarray(spread, jnp.bfloat16))
+    return jnp.transpose(slotted, (1, 0, 2))
 
 
 def body(populations, levels, refine_flags, new_owner):
@@ -447,29 +557,10 @@
     )
 
     state = run_steps(populations, rates)
+    outgoing = merge(leaving_block, state)
+    incoming = lax.all_to_all(outgoing, ("gx", "yz"), split_axis=0, concat_axis=0, tiled=True)
     pool = lay_out(state)
-    merge, spread = transfer_matrices()
-    coarse = jnp.einsum(
-        "bpf,fc->bpc",
-        pool,
-        jnp.asarray(merge, jnp.bfloat16),
-        preferred_element_type=jnp.float32,
-    ).astype(jnp.bfloat16)
-    outgoing = jnp.take(coarse, leaving_block, axis=0)
-    incoming = lax.all_to_all(outgoing, ("gx", "yz"), split_axis=0, concat_axis=0, tiled=True)
-    arrived = jnp.take(incoming, arrival_id // local, axis=0)
-    zero = jnp.zeros((), jnp.bfloat16)
-    kinds = arrival_kind[:, None, None]
-    both = jnp.concatenate(
-        [jnp.where(kinds == 1, arrived, zero), jnp.where(kinds == 2, arrived, zero)], axis=2
-    )
-    refined = jnp.einsum(
-        "bpc,cf->bpf",
-        both,
-        jnp.asarray(spread, jnp.bfloat16),
-        preferred_element_type=jnp.float32,
-    ).astype(jnp.bfloat16)
-    return fill(source, pool, refined)
+    return fill(source, arrival_id // local, arrival_kind, pool, incoming)
 
 
 def solution(mesh):

time: 84 us -> 63.5 us (0.76)
  waiting for transfers between devices: 20.1 us -> 6.13 us
  matrix products: 12 us -> 0 us
  local copies, waits for them, and re-layouts: 4.07 us -> 8.87 us
  Pallas kernels: 40.5 us -> 42.4 us
  other arithmetic: 3.5 us -> 2.3 us
    all_to_all x1, waiting for transfers between devices: 20.1 us -> 6.13 us  [body(): lax.all_to_all(outgoing, ('gx', 'yz'), split_axis=0, concat_axis=0, tiled...]
    dot_general x2 -> x0, matrix products: 12 us -> none  [the longest x1 8.34 us: body(): jnp.einsum('bpc,cf->bpf', both, jnp.asarray(spread, jnp.bfloat16), prefer...]
    unnamed x12 -> x20, local copies, waits for them, and re-layouts: 1.76 us -> 7.73 us
    pallas_call x0 -> x1, Pallas kernels: none -> 3.45 us  [merge(): pl.pallas_call(functools.partial(merge_kernel, nx, ny), out_shape=jax.Sha...]
    pallas_call x1, Pallas kernels: 12.4 us -> 10.7 us  [lay_out(): pl.pallas_call(functools.partial(layout_kernel, nx, ny, nz), out_shape=ja...]
    select_n x4 -> x1, other arithmetic: 1.18 us -> 0.01 us  [body(): return fill(source, arrival_id // local, arrival_kind, pool, incoming)]
    gather x2 -> x0, local copies, waits for them, and re-layouts: 1.17 us -> none  [the longest x1 0.6 us: body(): outgoing = jnp.take(coarse, leaving_block, axis=0)]
  transfers between devices with their start and end apart: 1 -> 1, of which waited for: 1 -> 1; matrix products, arithmetic and copies ran while one was open for 1% -> 1% of each run, Pallas kernels for 0% -> 17%
where the time goes in v2:
time: 63.5 us; the launch traced here: 63.1 us
  Pallas kernels  42.4 us (67%)
  local copies, waits for them, and re-layouts  8.87 us (14%)
  waiting for transfers between devices  6.13 us (10%)
  starting transfers between devices  3.23 us (5%)
  other arithmetic  2.3 us (4%)
    pallas_call x1, Pallas kernels, run_steps(): pl.pallas_call(functools.partial(steps_kernel, nx, ny), out_shape=jax.Sha...  21.5 us
    pallas_call x1, Pallas kernels, lay_out(): pl.pallas_call(functools.partial(layout_kernel, nx, ny, nz), out_shape=ja...  10.7 us
    unnamed x20, local copies, waits for them, and re-layouts  7.73 us
    pallas_call x1, Pallas kernels, fill(): pl.pallas_call(fill_kernel, out_shape=jax.ShapeDtypeStruct((POPS, CAP, BS...  6.76 us
    all_to_all x1, waiting for transfers between devices, body(): lax.all_to_all(outgoing, ('gx', 'yz'), split_axis=0, concat_axis=0, tiled...  6.13 us
    pallas_call x1, Pallas kernels, merge(): pl.pallas_call(functools.partial(merge_kernel, nx, ny), out_shape=jax.Sha...  3.45 us
    all_to_all x1, starting transfers between devices, body(): lax.all_to_all(outgoing, ('gx', 'yz'), split_axis=0, concat_axis=0, tiled...  3.23 us
  transfers between devices with their start and end apart: 1, of which 1 were waited for; matrix products, arithmetic and copies ran while one was open for 1% of the time, Pallas kernels for 17%

profile of v2, /device:TPU:1, one launch (start us, length us, event | category | flops | bytes accessed | tf_op | source)
XLA Modules:
  0.0 63.1 jit_solution(17934073119585226557)
XLA Ops:
  0.0 0.8 %add_divide_fusion = f32[16]{0:T(128)S(1)} fusion(s32[512]{0:T(512)} %param.9, s32[]{:T(128)S(6)} %select_n.51), kind=kLoop, calls=%fused_computation.29 | loop fusion | flops 48 | bytes 132 | tf_op jit(solution)/shard_map/div | solution.py:524
  0.8 0.1 div.23
  0.8 0.8 %dynamic-slice_compare_fusion = pred[16]{0:T(512)(128)(4,1)S(1)} fusion(s32[512]{0:T(512)} %param.10, s32[]{:T(128)S(6)} %select_n.51), kind=kLoop, calls=%fused_computation.28 | loop fusion | flops 16 | bytes 84 | tf_op jit(solution)/shard_map/ne | solution.py:552
  1.6 0.8 %dynamic_slice.11 = s32[16]{0:T(128)S(1)} dynamic-slice(s32[512]{0:T(512)} %param.11, s32[]{:T(128)S(6)} %select_n.51), dynamic_slice_sizes={16} | dynamic-slice | bytes 132 | tf_op jit(solution)/shard_map/dynamic_slice | solution.py:551
  2.4 0.1 copy.11
  2.4 0.1 broadcast_in_dim.85
  2.5 0.1 reshape.25
  2.6 0.1 copy.12.rate_ref
  2.7 0.1 select_reduce_fusion.2.leaving_ref
  2.8 0.0 copy-start.3
  2.8 1.7 %copy-done.3 = bf16[19,16,32,128]{3,2,1,0:T(8,128)(2,1)S(1)} copy-done((bf16[19,16,32,128]{3,2,1,0:T(8,128)(2,1)S(1)}, bf16[19,16,32,128]{3,2,1,0:T(8,128)(2,1)}, u32[]{:S(2)}) %copy-start.3) | copy-done | bytes 2490392
  4.5 0.0 copy-start.4
  4.5 0.0 copy-start.6
  4.5 21.5 %steps.1.state_ref = bf16[19,16,32,128]{3,2,1,0:T(8,128)(2,1)S(1)} custom-call(bf16[19,16,32,128]{3,2,1,0:T(8,128)(2,1)S(1)} %copy-done.3, f32[32,128]{1,0:T(8,128)S(1)} %copy.12.rate_ref), custom_call_target="tpu_custom_call" | custom-call | tf_op jit(solution)/shard_map/steps/pallas_call | solution.py:248
  26.0 0.0 copy-done.4
  26.0 0.0 copy-done.6
  26.1 0.0 copy-start.8
  26.1 0.0 copy-start.9
  26.1 3.5 %merge.1 = bf16[32,19,512]{2,1,0:T(8,128)(2,1)S(1)} custom-call(s32[32]{0:T(128)S(1)} %select_reduce_fusion.2.leaving_ref, bf16[19,16,32,128]{3,2,1,0:T(8,128)(2,1)S(1)} %steps.1.state_ref, bf16[512,128]{1,0:T(8,128)(2,1)S(1)} %copy-done.6, bf16[1024,1024]{1,0:T(8,128)(2,1)S(1)} %copy-done.4), custom_call_target="tpu_custom_call" | custom-call | tf_op jit(solution)/shard_map/merge/pallas_call | solution.py:393
  29.5 0.0 copy-start.2
  29.5 0.9 %copy-done.2 = bf16[32,19,512]{2,1,0:T(8,128)(2,1)} copy-done((bf16[32,19,512]{2,1,0:T(8,128)(2,1)}, bf16[32,19,512]{2,1,0:T(8,128)(2,1)S(1)}, u32[]{:S(2)}) %copy-start.2) | copy-done | bytes 622616
  30.4 3.2 %all-to-all-start = ((bf16[32,19,512]{2,1,0:T(8,128)(2,1)}), bf16[32,19,512]{2,1,0:T(8,128)(2,1)S(1)}, u32[]{:S(2)}, u32[]{:S(2)}) async-start(bf16[32,19,512]{2,1,0:T(8,128)(2,1)} %copy-done.2), calls=%async_computation | async-start | bytes 1572864 | tf_op jit(solution)/shard_map/all_to_all | solution.py:561
  33.7 0.0 copy-done.8
  33.7 0.1 convert_reduce_fusion
  33.8 0.0 copy-done.9
  33.8 0.1 select_reduce_fusion.1
  34.0 0.1 convert_reduce_fusion.1
  34.1 0.1 select_reduce_fusion.3
  34.2 0.1 fusion.2
  34.4 0.0 copy-start.7
  34.4 1.6 %copy-done.7 = bf16[1024,1024]{1,0:T(8,128)(2,1)S(1)} copy-done((bf16[1024,1024]{1,0:T(8,128)(2,1)S(1)}, bf16[1024,1024]{1,0:T(8,128)(2,1)}, u32[]{:S(2)}) %copy-start.7) | copy-done | bytes 2097176
  36.0 0.0 copy-start.5
  36.0 10.7 %layout.1.pool_ref = bf16[16,19,4096]{2,1,0:T(8,128)(2,1)S(1)} custom-call(bf16[19,16,32,128]{3,2,1,0:T(8,128)(2,1)S(1)} %steps.1.state_ref, bf16[1024,1024]{1,0:T(8,128)(2,1)S(1)} %copy-done.7), custom_call_target="tpu_custom_call" | custom-call | flops 2550136832 | bytes 9961472 | tf_op jit(solution)/shard_map/layout/pallas_call | solution.py:314
  46.7 0.0 copy-start
  46.7 1.7 %copy-done = bf16[16,19,4096]{2,1,0:T(8,128)(2,1)} copy-done((bf16[16,19,4096]{2,1,0:T(8,128)(2,1)}, bf16[16,19,4096]{2,1,0:T(8,128)(2,1)S(1)}, u32[]{:S(2)}) %copy-start) | copy-done | bytes 2490392
  48.4 6.1 %all-to-all-done.incoming_ref = bf16[32,19,512]{2,1,0:T(8,128)(2,1)S(1)} async-done(((bf16[32,19,512]{2,1,0:T(8,128)(2,1)}), bf16[32,19,512]{2,1,0:T(8,128)(2,1)S(1)}, u32[]{:S(2)}, u32[]{:S(2)}) %all-to-all-start) | async-done | bytes 622624 | tf_op jit(solution)/shard_map/all_to_all | solution.py:561
  54.5 0.0 copy-done.5
  54.5 0.0 copy-start.1
  54.5 1.9 %copy-done.1 = bf16[16,19,4096]{2,1,0:T(8,128)(2,1)S(1)} copy-done((bf16[16,19,4096]{2,1,0:T(8,128)(2,1)S(1)}, bf16[16,19,4096]{2,1,0:T(8,128)(2,1)}, u32[]{:S(2)}) %copy-start.1) | copy-done | bytes 2490392
  56.4 6.8 %fill.1 = bf16[19,24,4096]{2,1,0:T(8,128)(2,1)} custom-call(s32[24]{0:T(128)S(1)} %fusion.8.source_ref, s32[16]{0:T(128)S(1)} %and_select_fusion.origin_ref, s32[16]{0:T(128)S(1)} %get-tuple-element.7.kind_ref, bf16[16,19,4096]{2,1,0:T(8,128)(2,1)S(1)} %copy-done.1, bf16[32,19,512]{2,1,0:T(8,128)(2,1)S(1)} %all-to-all-done.incoming_ref, ...), custom_call_target="tpu_custom_call" | custom-call | tf_op jit(solution)/shard_map/fill/pallas_call | solution.py:492
  (5 shorter events, 0.0 us)
Async XLA Ops:
  2.8 1.7 %copy-start.3 = (bf16[19,16,32,128]{3,2,1,0:T(8,128)(2,1)S(1)}, bf16[19,16,32,128]{3,2,1,0:T(8,128)(2,1)}, u32[]{:S(2)}) copy-start(bf16[19,16,32,128]{3,2,1,0:T(8,128)(2,1)} %pop_ref.1) | copy-start | bytes 7471108
  4.5 21.5 %copy-start.4 = (bf16[1024,1024]{1,0:T(8,128)(2,1)S(1)}, bf16[1024,1024]{1,0:T(8,128)(2,1)}, u32[]{:S(2)}) copy-start(bf16[1024,1024]{1,0:T(8,128)(2,1)} %constant.61.clone.select_ref) | copy-start | bytes 6291460
  4.5 21.6 %copy-start.6 = (bf16[512,128]{1,0:T(8,128)(2,1)S(1)}, bf16[512,128]{1,0:T(8,128)(2,1)}, u32[]{:S(2)}) copy-start(bf16[512,128]{1,0:T(8,128)(2,1)} %constant.60.clone.shrink_ref) | copy-start | bytes 393220
  26.1 7.6 %copy-start.8 = (s32[512]{0:T(512)S(1)}, s32[512]{0:T(512)}, u32[]{:S(2)}) copy-start(s32[512]{0:T(512)} %param.11) | copy-start | bytes 6148
  26.1 7.8 %copy-start.9 = (s32[512]{0:T(512)S(1)}, s32[512]{0:T(512)}, u32[]{:S(2)}) copy-start(s32[512]{0:T(512)} %param.10) | copy-start | bytes 6148
  29.5 0.9 %copy-start.2 = (bf16[32,19,512]{2,1,0:T(8,128)(2,1)}, bf16[32,19,512]{2,1,0:T(8,128)(2,1)S(1)}, u32[]{:S(2)}) copy-start(bf16[32,19,512]{2,1,0:T(8,128)(2,1)S(1)} %merge.1) | copy-start | bytes 1867780
  30.4 24.1 %all-to-all-start = ((bf16[32,19,512]{2,1,0:T(8,128)(2,1)}), bf16[32,19,512]{2,1,0:T(8,128)(2,1)S(1)}, u32[]{:S(2)}, u32[]{:S(2)}) async-start(bf16[32,19,512]{2,1,0:T(8,128)(2,1)} %copy-done.2), calls=%async_computation | async-start | bytes 1572864 | tf_op jit(solution)/shard_map/all_to_all | solution.py:561
  34.4 1.6 %copy-start.7 = (bf16[1024,1024]{1,0:T(8,128)(2,1)S(1)}, bf16[1024,1024]{1,0:T(8,128)(2,1)}, u32[]{:S(2)}) copy-start(bf16[1024,1024]{1,0:T(8,128)(2,1)} %constant.62.clone.select_ref) | copy-start | bytes 6291460
  36.0 18.5 %copy-start.5 = (bf16[256,512]{1,0:T(8,128)(2,1)S(1)}, bf16[256,512]{1,0:T(8,128)(2,1)}, u32[]{:S(2)}) copy-start(bf16[256,512]{1,0:T(8,128)(2,1)} %constant.63.clone.spread_ref) | copy-start | bytes 786436
  46.7 1.7 %copy-start = (bf16[16,19,4096]{2,1,0:T(8,128)(2,1)}, bf16[16,19,4096]{2,1,0:T(8,128)(2,1)S(1)}, u32[]{:S(2)}) copy-start(bf16[16,19,4096]{2,1,0:T(8,128)(2,1)S(1)} %layout.1.pool_ref) | copy-start | bytes 7471108
  54.5 1.9 %copy-start.1 = (bf16[16,19,4096]{2,1,0:T(8,128)(2,1)S(1)}, bf16[16,19,4096]{2,1,0:T(8,128)(2,1)}, u32[]{:S(2)}) copy-start(bf16[16,19,4096]{2,1,0:T(8,128)(2,1)} %copy-done) | copy-start | bytes 7471108

commit v3 on v2

--- a/solution.py
+++ b/solution.py
@@ -133,21 +133,20 @@
     barrier = pltpu.get_barrier_semaphore()
     for offset in NEIGHBOURS:
         pl.semaphore_signal(barrier, inc=1, device_id=device(offset), device_id_type=MESH)
-    lane = lax.broadcasted_iota(jnp.int32, (BS, nz), 1)
-
-    def put(target, x, start, collided):
+    def put(target, x, start, count, collided):
         for p in range(POPS):
             rounded = collided[p].astype(jnp.bfloat16).astype(jnp.float32)
-            target[p, x + 1, PAD + start : PAD + start + BS, :] = rounded
-
-    def gather(source, x, start):
+            target[p, x + 1, PAD + start : PAD + start + count, :] = rounded
+
+    def gather(source, x, start, count):
+        lane = lax.broadcasted_iota(jnp.int32, (count, nz), 1)
         values = []
         for p in range(POPS):
             dx, dy, dz = VELOCITY[p]
             low = PAD + start - dy
-            value = source[p, x + 1 - dx, low : low + BS, :]
+            value = source[p, x + 1 - dx, low : low + count, :]
             if dz != 0:
-                mirror = source[OPPOSITE[p], x + 1, PAD + start : PAD + start + BS, :]
+                mirror = source[OPPOSITE[p], x + 1, PAD + start : PAD + start + count, :]
                 if dz == 1:
                     value = jnp.where(lane == 0, mirror, pltpu.roll(value, 1, axis=1))
                 else:
@@ -155,13 +154,35 @@
             values.append(value)
         return values
 
-    def exchange(step, field):
+    def send(step, first_index, pairs):
+        copies = []
+        for n, pair in enumerate(pairs, first_index):
+            copy = pltpu.make_async_remote_copy(
+                src_ref=pair[0],
+                dst_ref=pair[1],
+                send_sem=send_sem.at[step, n],
+                recv_sem=recv_sem.at[step, n],
+                device_id=device(NEIGHBOURS[n]),
+                device_id_type=MESH,
+            )
+            copy.start()
+            copies.append(copy)
+        return copies
+
+    def send_x(step, field):
         for side in range(2):
             plane = nx if side == 0 else 1
-            row = PAD + ny - 1 if side == 0 else PAD
             for k, p in enumerate(CROSSING[side]):
                 x_send[step, side, k] = field[p, plane, PAD : PAD + ny, :]
-
+        for c, (dx, dy) in enumerate(CORNERS):
+            low = ny if dy == 1 else PAD
+            c_send[step, c] = field[7 + c, nx if dx == 1 else 1, low : low + PAD, :]
+        if step == 0:
+            pl.semaphore_wait(barrier, len(NEIGHBOURS))
+        copies = send(step, 0, [(x_send.at[step, n], x_recv.at[step, n]) for n in range(2)])
+        return copies + send(step, 4, [(c_send.at[step, n], c_recv.at[step, n]) for n in range(4)])
+
+    def send_y(step, field):
         def pack(x, carry):
             for side in range(2):
                 row = PAD + ny - 1 if side == 0 else PAD
@@ -170,34 +191,21 @@
             return carry
 
         lax.fori_loop(0, nx, pack, 0)
-        for c, (dx, dy) in enumerate(CORNERS):
-            low = ny if dy == 1 else PAD
-            c_send[step, c] = field[7 + c, nx if dx == 1 else 1, low : low + PAD, :]
-        if step == 0:
-            pl.semaphore_wait(barrier, len(NEIGHBOURS))
-        copies = []
-        for n, offset in enumerate(NEIGHBOURS):
-            if n < 2:
-                pair = (x_send.at[step, n], x_recv.at[step, n])
-            elif n < 4:
-                pair = (y_send.at[step, n - 2], y_recv.at[step, n - 2])
-            else:
-                pair = (c_send.at[step, n - 4], c_recv.at[step, n - 4])
-            copy = pltpu.make_async_remote_copy(
-                src_ref=pair[0],
-                dst_ref=pair[1],
-                send_sem=send_sem.at[step, n],
-                recv_sem=recv_sem.at[step, n],
-                device_id=device(offset),
-                device_id_type=MESH,
-            )
-            copy.start()
-            copies.append(copy)
+        return send(step, 2, [(y_send.at[step, n], y_recv.at[step, n]) for n in range(2)])
+
+    def take_x(step, field, copies):
         for copy in copies:
             copy.wait()
         for side in range(2):
             for k, p in enumerate(CROSSING[side]):
                 field[p, 0 if side == 0 else nx + 1, PAD : PAD + ny, :] = x_recv[step, side, k]
+        for c, (dx, dy) in enumerate(CORNERS):
+            low = 0 if dy == 1 else PAD + ny
+            field[7 + c, 0 if dx == 1 else nx + 1, low : low + PAD, :] = c_recv[step, c]
+
+    def take_y(step, field, copies):
+        for copy in copies:
+            copy.wait()
 
         def unpack(x, carry):
             for side in range(2):
@@ -207,36 +215,46 @@
             return carry
 
         lax.fori_loop(0, nx, unpack, 0)
-        for c, (dx, dy) in enumerate(CORNERS):
-            low = 0 if dy == 1 else PAD + ny
-            field[7 + c, 0 if dx == 1 else nx + 1, low : low + PAD, :] = c_recv[step, c]
-
-    starts = range(0, ny, BS)
-
-    def begin(x, carry):
+
+    def begin(x):
+        for start in range(0, ny, BS):
+            values = [pop_ref[p, x, start : start + BS, :].astype(jnp.float32) for p in range(POPS)]
+            put(first, x, start, BS, collide(values, rate_ref[start : start + BS, :]))
+
+    def middle(x, starts):
         for start in starts:
-            values = [pop_ref[p, x, start : start + BS, :].astype(jnp.float32) for p in range(POPS)]
-            put(first, x, start, collide(values, rate_ref[start : start + BS, :]))
-        return carry
-
-    def middle(x, carry):
-        for start in starts:
-            values = gather(first, x, start)
-            put(second, x, start, collide(values, rate_ref[start : start + BS, :]))
-        return carry
-
-    def finish(x, carry):
-        for start in starts:
-            values = gather(second, x, start)
+            values = gather(first, x, start, 8)
+            put(second, x, start, 8, collide(values, rate_ref[start : start + 8, :]))
+
+    def finish(x):
+        for start in range(0, ny, BS):
+            values = gather(second, x, start, BS)
             for p in range(POPS):
                 out_ref[p, x, start : start + BS, :] = values[p].astype(jnp.bfloat16)
-        return carry
-
-    lax.fori_loop(0, nx, begin, 0)
-    exchange(0, first)
-    lax.fori_loop(0, nx, middle, 0)
-    exchange(1, second)
-    lax.fori_loop(0, nx, finish, 0)
+
+    def sweep(low, high, work):
+        def one(x, carry):
+            work(x)
+            return carry
+
+        lax.fori_loop(low, high, one, 0)
+
+    inner = range(8, ny - 8, 8)
+    outer = (0, ny - 8)
+    sweep(0, 2, lambda i: begin(i * (nx - 1)))
+    x_copies = send_x(0, first)
+    sweep(1, nx - 1, begin)
+    y_copies = send_y(0, first)
+    take_x(0, first, x_copies)
+    sweep(0, nx, lambda x: middle(x, inner))
+    take_y(0, first, y_copies)
+    sweep(0, 2, lambda i: middle(i * (nx - 1), outer))
+    x_copies = send_x(1, second)
+    sweep(1, nx - 1, lambda x: middle(x, outer))
+    y_copies = send_y(1, second)
+    take_x(1, second, x_copies)
+    take_y(1, second, y_copies)
+    sweep(0, nx, finish)
 
 
 def run_steps(populations, rates):
@@ -407,8 +425,21 @@
 
 
 def fill_kernel(
-    source_ref, origin_ref, kind_ref, pool_ref, incoming_ref, spread_ref, out_ref, held, packed, wide
+    source_ref,
+    origin_ref,
+    kind_ref,
+    pool_source,
+    incoming_ref,
+    spread_ref,
+    out_ref,
+    held,
+    packed,
+    wide,
+    pool_ref,
+    pool_sem,
 ):
+    fetch = pltpu.make_async_copy(pool_source, pool_ref, pool_sem)
+    fetch.start()
     blocks = pool_ref.shape[0]
     arrivals = origin_ref.shape[0]
     packed[...] = jnp.zeros_like(packed)
@@ -434,6 +465,7 @@
         return carry
 
     lax.fori_loop(0, arrivals // 4, expand, 0)
+    fetch.wait()
 
     def place(slot, carry):
         source = source_ref[slot]
@@ -493,12 +525,15 @@
         fill_kernel,
         out_shape=jax.ShapeDtypeStruct((POPS, CAP, BS**3), jnp.bfloat16),
         in_specs=[pl.BlockSpec(memory_space=pltpu.SMEM)] * 3
-        + [pl.BlockSpec(memory_space=pltpu.VMEM)] * 3,
+        + [pl.BlockSpec(memory_space=pl.ANY)]
+        + [pl.BlockSpec(memory_space=pltpu.VMEM)] * 2,
         out_specs=pl.BlockSpec(memory_space=pltpu.VMEM),
         scratch_shapes=[
             pltpu.VMEM((LANES, POPS * CAP, 128), jnp.float32),
             pltpu.VMEM((count * QUADS, ROWS, 256), jnp.bfloat16),
             pltpu.VMEM((count * QUADS, ROWS, 512), jnp.float32),
+            pltpu.VMEM(pool.shape, jnp.bfloat16),
+            pltpu.SemaphoreType.DMA(()),
         ],
         compiler_params=pltpu.CompilerParams(vmem_limit_bytes=48 * 2**20),
         name="fill",

time: 63.5 us -> 63.8 us (level)
  starting transfers between devices: 3.23 us -> 5.27 us
  Pallas kernels: 42.4 us -> 40.6 us
    pallas_call x1, Pallas kernels: 21.5 us -> 19.4 us  [run_steps(): pl.pallas_call(functools.partial(steps_kernel, nx, ny), out_shape=jax.Sha...]
    all_to_all x1, starting transfers between devices: 3.23 us -> 5.27 us  [body(): lax.all_to_all(outgoing, ('gx', 'yz'), split_axis=0, concat_axis=0, tiled...]
where the time goes in v3:
time: 63.8 us; the launch traced here: 63.3 us
  Pallas kernels  40.6 us (64%)
  local copies, waits for them, and re-layouts  8.87 us (14%)
  waiting for transfers between devices  6.13 us (10%)
  starting transfers between devices  5.27 us (8%)
  other arithmetic  2.3 us (4%)
    pallas_call x1, Pallas kernels, run_steps(): pl.pallas_call(functools.partial(steps_kernel, nx, ny), out_shape=jax.Sha...  19.4 us
    pallas_call x1, Pallas kernels, lay_out(): pl.pallas_call(functools.partial(layout_kernel, nx, ny, nz), out_shape=ja...  10.7 us
    unnamed x20, local copies, waits for them, and re-layouts  7.73 us
    pallas_call x1, Pallas kernels, fill(): pl.pallas_call(fill_kernel, out_shape=jax.ShapeDtypeStruct((POPS, CAP, BS...  7.04 us
    all_to_all x1, waiting for transfers between devices, body(): lax.all_to_all(outgoing, ('gx', 'yz'), split_axis=0, concat_axis=0, tiled...  6.13 us
    all_to_all x1, starting transfers between devices, body(): lax.all_to_all(outgoing, ('gx', 'yz'), split_axis=0, concat_axis=0, tiled...  5.27 us
    pallas_call x1, Pallas kernels, merge(): pl.pallas_call(functools.partial(merge_kernel, nx, ny), out_shape=jax.Sha...  3.45 us
  transfers between devices with their start and end apart: 1, of which 1 were waited for; matrix products, arithmetic and copies ran while one was open for 1% of the time, Pallas kernels for 17%

profile of v3, /device:TPU:1, one launch (start us, length us, event | category | flops | bytes accessed | tf_op | source)
XLA Modules:
  0.0 63.3 jit_solution(10612929233979592194)
XLA Ops:
  0.0 0.8 %add_divide_fusion = f32[16]{0:T(128)S(1)} fusion(s32[512]{0:T(512)} %param.9, s32[]{:T(128)S(6)} %select_n.51), kind=kLoop, calls=%fused_computation.29 | loop fusion | flops 48 | bytes 132 | tf_op jit(solution)/shard_map/div | solution.py:559
  0.8 0.1 div.23
  0.8 0.8 %dynamic-slice_compare_fusion = pred[16]{0:T(512)(128)(4,1)S(1)} fusion(s32[512]{0:T(512)} %param.10, s32[]{:T(128)S(6)} %select_n.51), kind=kLoop, calls=%fused_computation.28 | loop fusion | flops 16 | bytes 84 | tf_op jit(solution)/shard_map/ne | solution.py:587
  1.6 0.8 %dynamic_slice.11 = s32[16]{0:T(128)S(1)} dynamic-slice(s32[512]{0:T(512)} %param.11, s32[]{:T(128)S(6)} %select_n.51), dynamic_slice_sizes={16} | dynamic-slice | bytes 132 | tf_op jit(solution)/shard_map/dynamic_slice | solution.py:586
  2.4 0.1 copy.11
  2.4 0.1 broadcast_in_dim.85
  2.5 0.1 reshape.25
  2.6 0.1 copy.12.rate_ref
  2.7 0.1 select_reduce_fusion.2.leaving_ref
  2.8 0.0 copy-start.3
  2.8 1.7 %copy-done.3 = bf16[19,16,32,128]{3,2,1,0:T(8,128)(2,1)S(1)} copy-done((bf16[19,16,32,128]{3,2,1,0:T(8,128)(2,1)S(1)}, bf16[19,16,32,128]{3,2,1,0:T(8,128)(2,1)}, u32[]{:S(2)}) %copy-start.3) | copy-done | bytes 2490392
  4.5 0.0 copy-start.4
  4.5 0.0 copy-start.6
  4.5 19.4 %steps.1.state_ref = bf16[19,16,32,128]{3,2,1,0:T(8,128)(2,1)S(1)} custom-call(bf16[19,16,32,128]{3,2,1,0:T(8,128)(2,1)S(1)} %copy-done.3, f32[32,128]{1,0:T(8,128)S(1)} %copy.12.rate_ref), custom_call_target="tpu_custom_call" | custom-call | tf_op jit(solution)/shard_map/steps/pallas_call | solution.py:266
  23.9 0.0 copy-done.4
  23.9 0.0 copy-done.6
  23.9 0.0 copy-start.8
  24.0 0.0 copy-start.9
  24.0 3.4 %merge.1 = bf16[32,19,512]{2,1,0:T(8,128)(2,1)S(1)} custom-call(s32[32]{0:T(128)S(1)} %select_reduce_fusion.2.leaving_ref, bf16[19,16,32,128]{3,2,1,0:T(8,128)(2,1)S(1)} %steps.1.state_ref, bf16[512,128]{1,0:T(8,128)(2,1)S(1)} %copy-done.6, bf16[1024,1024]{1,0:T(8,128)(2,1)S(1)} %copy-done.4), custom_call_target="tpu_custom_call" | custom-call | tf_op jit(solution)/shard_map/merge/pallas_call | solution.py:411
  27.4 0.0 copy-start.2
  27.4 0.9 %copy-done.2 = bf16[32,19,512]{2,1,0:T(8,128)(2,1)} copy-done((bf16[32,19,512]{2,1,0:T(8,128)(2,1)}, bf16[32,19,512]{2,1,0:T(8,128)(2,1)S(1)}, u32[]{:S(2)}) %copy-start.2) | copy-done | bytes 622616
  28.3 5.3 %all-to-all-start = ((bf16[32,19,512]{2,1,0:T(8,128)(2,1)}), bf16[32,19,512]{2,1,0:T(8,128)(2,1)S(1)}, u32[]{:S(2)}, u32[]{:S(2)}) async-start(bf16[32,19,512]{2,1,0:T(8,128)(2,1)} %copy-done.2), calls=%async_computation | async-start | bytes 1572864 | tf_op jit(solution)/shard_map/all_to_all | solution.py:596
  33.6 0.0 copy-done.8
  33.6 0.1 convert_reduce_fusion
  33.8 0.0 copy-done.9
  33.8 0.1 select_reduce_fusion.1
  33.9 0.1 convert_reduce_fusion.1
  34.0 0.1 select_reduce_fusion.3
  34.1 0.1 fusion.2
  34.3 0.0 copy-start.7
  34.3 1.6 %copy-done.7 = bf16[1024,1024]{1,0:T(8,128)(2,1)S(1)} copy-done((bf16[1024,1024]{1,0:T(8,128)(2,1)S(1)}, bf16[1024,1024]{1,0:T(8,128)(2,1)}, u32[]{:S(2)}) %copy-start.7) | copy-done | bytes 2097176
  35.9 0.0 copy-start.5
  35.9 10.7 %layout.1.pool_source = bf16[16,19,4096]{2,1,0:T(8,128)(2,1)S(1)} custom-call(bf16[19,16,32,128]{3,2,1,0:T(8,128)(2,1)S(1)} %steps.1.state_ref, bf16[1024,1024]{1,0:T(8,128)(2,1)S(1)} %copy-done.7), custom_call_target="tpu_custom_call" | custom-call | flops 2550136832 | bytes 9961472 | tf_op jit(solution)/shard_map/layout/pallas_call | solution.py:332
  46.6 0.0 copy-start
  46.6 1.7 %copy-done = bf16[16,19,4096]{2,1,0:T(8,128)(2,1)} copy-done((bf16[16,19,4096]{2,1,0:T(8,128)(2,1)}, bf16[16,19,4096]{2,1,0:T(8,128)(2,1)S(1)}, u32[]{:S(2)}) %copy-start) | copy-done | bytes 2490392
  48.3 6.1 %all-to-all-done.incoming_ref = bf16[32,19,512]{2,1,0:T(8,128)(2,1)S(1)} async-done(((bf16[32,19,512]{2,1,0:T(8,128)(2,1)}), bf16[32,19,512]{2,1,0:T(8,128)(2,1)S(1)}, u32[]{:S(2)}, u32[]{:S(2)}) %all-to-all-start) | async-done | bytes 622624 | tf_op jit(solution)/shard_map/all_to_all | solution.py:596
  54.4 0.0 copy-done.5
  54.4 0.0 copy-start.1
  54.4 1.9 %copy-done.1 = bf16[16,19,4096]{2,1,0:T(8,128)(2,1)S(1)} copy-done((bf16[16,19,4096]{2,1,0:T(8,128)(2,1)S(1)}, bf16[16,19,4096]{2,1,0:T(8,128)(2,1)}, u32[]{:S(2)}) %copy-start.1) | copy-done | bytes 2490392
  56.3 7.0 %fill.1 = bf16[19,24,4096]{2,1,0:T(8,128)(2,1)} custom-call(s32[24]{0:T(128)S(1)} %fusion.8.source_ref, s32[16]{0:T(128)S(1)} %and_select_fusion.origin_ref, s32[16]{0:T(128)S(1)} %get-tuple-element.7.kind_ref, bf16[16,19,4096]{2,1,0:T(8,128)(2,1)S(1)} %copy-done.1, bf16[32,19,512]{2,1,0:T(8,128)(2,1)S(1)} %all-to-all-done.incoming_ref, ...), custom_call_target="tpu_custom_call" | custom-call | tf_op jit(solution)/shard_map/fill/pallas_call | solution.py:524
  (5 shorter events, 0.0 us)
Async XLA Ops:
  2.8 1.7 %copy-start.3 = (bf16[19,16,32,128]{3,2,1,0:T(8,128)(2,1)S(1)}, bf16[19,16,32,128]{3,2,1,0:T(8,128)(2,1)}, u32[]{:S(2)}) copy-start(bf16[19,16,32,128]{3,2,1,0:T(8,128)(2,1)} %pop_ref.1) | copy-start | bytes 7471108
  4.5 19.4 %copy-start.4 = (bf16[1024,1024]{1,0:T(8,128)(2,1)S(1)}, bf16[1024,1024]{1,0:T(8,128)(2,1)}, u32[]{:S(2)}) copy-start(bf16[1024,1024]{1,0:T(8,128)(2,1)} %constant.61.clone.select_ref) | copy-start | bytes 6291460
  4.5 19.4 %copy-start.6 = (bf16[512,128]{1,0:T(8,128)(2,1)S(1)}, bf16[512,128]{1,0:T(8,128)(2,1)}, u32[]{:S(2)}) copy-start(bf16[512,128]{1,0:T(8,128)(2,1)} %constant.60.clone.shrink_ref) | copy-start | bytes 393220
  23.9 9.6 %copy-start.8 = (s32[512]{0:T(512)S(1)}, s32[512]{0:T(512)}, u32[]{:S(2)}) copy-start(s32[512]{0:T(512)} %param.11) | copy-start | bytes 6148
  24.0 9.8 %copy-start.9 = (s32[512]{0:T(512)S(1)}, s32[512]{0:T(512)}, u32[]{:S(2)}) copy-start(s32[512]{0:T(512)} %param.10) | copy-start | bytes 6148
  27.4 0.9 %copy-start.2 = (bf16[32,19,512]{2,1,0:T(8,128)(2,1)}, bf16[32,19,512]{2,1,0:T(8,128)(2,1)S(1)}, u32[]{:S(2)}) copy-start(bf16[32,19,512]{2,1,0:T(8,128)(2,1)S(1)} %merge.1) | copy-start | bytes 1867780
  28.3 26.1 %all-to-all-start = ((bf16[32,19,512]{2,1,0:T(8,128)(2,1)}), bf16[32,19,512]{2,1,0:T(8,128)(2,1)S(1)}, u32[]{:S(2)}, u32[]{:S(2)}) async-start(bf16[32,19,512]{2,1,0:T(8,128)(2,1)} %copy-done.2), calls=%async_computation | async-start | bytes 1572864 | tf_op jit(solution)/shard_map/all_to_all | solution.py:596
  34.3 1.6 %copy-start.7 = (bf16[1024,1024]{1,0:T(8,128)(2,1)S(1)}, bf16[1024,1024]{1,0:T(8,128)(2,1)}, u32[]{:S(2)}) copy-start(bf16[1024,1024]{1,0:T(8,128)(2,1)} %constant.62.clone.select_ref) | copy-start | bytes 6291460
  35.9 18.5 %copy-start.5 = (bf16[256,512]{1,0:T(8,128)(2,1)S(1)}, bf16[256,512]{1,0:T(8,128)(2,1)}, u32[]{:S(2)}) copy-start(bf16[256,512]{1,0:T(8,128)(2,1)} %constant.63.clone.spread_ref) | copy-start | bytes 786436
  46.6 1.7 %copy-start = (bf16[16,19,4096]{2,1,0:T(8,128)(2,1)}, bf16[16,19,4096]{2,1,0:T(8,128)(2,1)S(1)}, u32[]{:S(2)}) copy-start(bf16[16,19,4096]{2,1,0:T(8,128)(2,1)S(1)} %layout.1.pool_source) | copy-start | bytes 7471108
  54.4 1.9 %copy-start.1 = (bf16[16,19,4096]{2,1,0:T(8,128)(2,1)S(1)}, bf16[16,19,4096]{2,1,0:T(8,128)(2,1)}, u32[]{:S(2)}) copy-start(bf16[16,19,4096]{2,1,0:T(8,128)(2,1)} %copy-done) | copy-start | bytes 7471108

commit v4 on v3

--- a/solution.py
+++ b/solution.py
@@ -535,7 +535,7 @@
             pltpu.VMEM(pool.shape, jnp.bfloat16),
             pltpu.SemaphoreType.DMA(()),
         ],
-        compiler_params=pltpu.CompilerParams(vmem_limit_bytes=48 * 2**20),
+        compiler_params=pltpu.CompilerParams(vmem_limit_bytes=61 * 2**20),
         name="fill",
     )(source, origin, kinds, pool, incoming, jnp.asarray(spread, jnp.bfloat16))
     return jnp.transpose(slotted, (1, 0, 2))

time: 63.8 us -> 63.6 us (level)
  local copies, waits for them, and re-layouts: 8.87 us -> 6.99 us
  Pallas kernels: 40.6 us -> 42.4 us
  other arithmetic: 2.3 us -> 3.92 us
  waiting for transfers between devices: 6.13 us -> 4.54 us
    unnamed x20 -> x16, local copies, waits for them, and re-layouts: 7.73 us -> 5.86 us
    all_to_all x1, waiting for transfers between devices: 6.13 us -> 4.54 us  [body(): lax.all_to_all(outgoing, ('gx', 'yz'), split_axis=0, concat_axis=0, tiled...]
    pallas_call x1, Pallas kernels: 7.04 us -> 8 us  [fill(): pl.pallas_call(fill_kernel, out_shape=jax.ShapeDtypeStruct((POPS, CAP, BS...]
    pallas_call x1, Pallas kernels: 3.45 us -> 4.33 us  [merge(): pl.pallas_call(functools.partial(merge_kernel, nx, ny), out_shape=jax.Sha...]
  transfers between devices with their start and end apart: 1 -> 1, of which waited for: 1 -> 1; matrix products, arithmetic and copies ran while one was open for 1% -> 4% of each run, Pallas kernels for 17% -> 17%
where the time goes in v4:
time: 63.6 us; the launch traced here: 63.3 us
  Pallas kernels  42.4 us (67%)
  local copies, waits for them, and re-layouts  6.99 us (11%)
  starting transfers between devices  5.27 us (8%)
  waiting for transfers between devices  4.54 us (7%)
  other arithmetic  3.92 us (6%)
    pallas_call x1, Pallas kernels, run_steps(): pl.pallas_call(functools.partial(steps_kernel, nx, ny), out_shape=jax.Sha...  19.4 us
    pallas_call x1, Pallas kernels, lay_out(): pl.pallas_call(functools.partial(layout_kernel, nx, ny, nz), out_shape=ja...  10.7 us
    pallas_call x1, Pallas kernels, fill(): pl.pallas_call(fill_kernel, out_shape=jax.ShapeDtypeStruct((POPS, CAP, BS...  8 us
    unnamed x16, local copies, waits for them, and re-layouts  5.86 us
    all_to_all x1, starting transfers between devices, body(): lax.all_to_all(outgoing, ('gx', 'yz'), split_axis=0, concat_axis=0, tiled...  5.27 us
    all_to_all x1, waiting for transfers between devices, body(): lax.all_to_all(outgoing, ('gx', 'yz'), split_axis=0, concat_axis=0, tiled...  4.54 us
    pallas_call x1, Pallas kernels, merge(): pl.pallas_call(functools.partial(merge_kernel, nx, ny), out_shape=jax.Sha...  4.33 us
  transfers between devices with their start and end apart: 1, of which 1 were waited for; matrix products, arithmetic and copies ran while one was open for 4% of the time, Pallas kernels for 17%

profile of v4, /device:TPU:1, one launch (start us, length us, event | category | flops | bytes accessed | tf_op | source)
XLA Modules:
  0.0 63.3 jit_solution(11041919807089869872)
XLA Ops:
  0.0 0.8 %add_divide_fusion = f32[16]{0:T(128)S(1)} fusion(s32[512]{0:T(512)} %param.9, s32[]{:T(128)S(6)} %select_n.51), kind=kLoop, calls=%fused_computation.29 | loop fusion | flops 48 | bytes 132 | tf_op jit(solution)/shard_map/div | solution.py:559
  0.8 0.1 div.23
  0.8 0.8 %dynamic-slice_compare_fusion = pred[16]{0:T(512)(128)(4,1)S(1)} fusion(s32[512]{0:T(512)} %param.10, s32[]{:T(128)S(6)} %select_n.51), kind=kLoop, calls=%fused_computation.28 | loop fusion | flops 16 | bytes 84 | tf_op jit(solution)/shard_map/ne | solution.py:587
  1.6 0.8 %dynamic_slice.11 = s32[16]{0:T(128)S(1)} dynamic-slice(s32[512]{0:T(512)} %param.11, s32[]{:T(128)S(6)} %select_n.51), dynamic_slice_sizes={16} | dynamic-slice | bytes 132 | tf_op jit(solution)/shard_map/dynamic_slice | solution.py:586
  2.4 0.1 copy.11
  2.4 0.1 broadcast_in_dim.85
  2.5 0.1 reshape.25
  2.6 0.1 copy.12.rate_ref
  2.7 0.1 select_reduce_fusion.2.leaving_ref
  2.8 0.0 copy-start.1
  2.8 1.7 %copy-done.1 = bf16[19,16,32,128]{3,2,1,0:T(8,128)(2,1)S(1)} copy-done((bf16[19,16,32,128]{3,2,1,0:T(8,128)(2,1)S(1)}, bf16[19,16,32,128]{3,2,1,0:T(8,128)(2,1)}, u32[]{:S(2)}) %copy-start.1) | copy-done | bytes 2490392
  4.5 0.0 copy-start.2
  4.5 0.0 copy-start.3
  4.5 19.4 %steps.1.state_ref = bf16[19,16,32,128]{3,2,1,0:T(8,128)(2,1)S(1)} custom-call(bf16[19,16,32,128]{3,2,1,0:T(8,128)(2,1)S(1)} %copy-done.1, f32[32,128]{1,0:T(8,128)S(1)} %copy.12.rate_ref), custom_call_target="tpu_custom_call" | custom-call | tf_op jit(solution)/shard_map/steps/pallas_call | solution.py:266
  23.9 0.0 copy-done.2
  23.9 0.0 copy-done.3
  23.9 0.0 copy-start.6
  24.0 0.0 copy-start.7
  24.0 4.3 %merge.1 = bf16[32,19,512]{2,1,0:T(8,128)(2,1)} custom-call(s32[32]{0:T(128)S(1)} %select_reduce_fusion.2.leaving_ref, bf16[19,16,32,128]{3,2,1,0:T(8,128)(2,1)S(1)} %steps.1.state_ref, bf16[512,128]{1,0:T(8,128)(2,1)S(1)} %copy-done.3, bf16[1024,1024]{1,0:T(8,128)(2,1)S(1)} %copy-done.2), custom_call_target="tpu_custom_call" | custom-call | tf_op jit(solution)/shard_map/merge/pallas_call | solution.py:411
  28.3 5.3 %all-to-all-start = ((bf16[32,19,512]{2,1,0:T(8,128)(2,1)}), bf16[32,19,512]{2,1,0:T(8,128)(2,1)S(1)}, u32[]{:S(2)}, u32[]{:S(2)}) async-start(bf16[32,19,512]{2,1,0:T(8,128)(2,1)} %merge.1), calls=%async_computation | async-start | bytes 1572864 | tf_op jit(solution)/shard_map/all_to_all | solution.py:596
  33.6 0.0 copy-done.6
  33.6 0.1 convert_reduce_fusion
  33.7 0.0 copy-done.7
  33.8 0.1 select_reduce_fusion.1
  33.9 0.1 convert_reduce_fusion.1
  34.0 0.7 %select_reduce_fusion.3 = (s32[16]{0:T(128)}, s32[16]{0:T(128)S(1)}) fusion(s32[24]{0:T(128)S(1)} %get-tuple-element.5, s32[24]{0:T(128)S(1)} %convert_reduce_fusion.1, pred[24]{0:T(512)(128)(4,1)S(1)} %broadcast_compare_fusion.1, s32[24]{0:T(128)S(1)} %get-tuple-element.6), kind=kLoop, calls=%fused_computation.13 | loop fusion | flops 2272 | bytes 440 | tf_op jit(solution)/shard_map/reduce_sum | solution.py:578
  34.7 0.1 fusion.2
  34.8 0.5 and_select_fusion.origin_ref
  35.3 0.5 fusion.8.source_ref
  35.9 0.0 copy-start.4
  35.9 1.6 %copy-done.4 = bf16[1024,1024]{1,0:T(8,128)(2,1)S(1)} copy-done((bf16[1024,1024]{1,0:T(8,128)(2,1)S(1)}, bf16[1024,1024]{1,0:T(8,128)(2,1)}, u32[]{:S(2)}) %copy-start.4) | copy-done | bytes 2097176
  37.5 10.7 %layout.1.pool_source = bf16[16,19,4096]{2,1,0:T(8,128)(2,1)S(1)} custom-call(bf16[19,16,32,128]{3,2,1,0:T(8,128)(2,1)S(1)} %steps.1.state_ref, bf16[1024,1024]{1,0:T(8,128)(2,1)S(1)} %copy-done.4), custom_call_target="tpu_custom_call" | custom-call | flops 2550136832 | bytes 9961472 | tf_op jit(solution)/shard_map/layout/pallas_call | solution.py:332
  48.2 0.0 copy-start
  48.2 1.7 %copy-done = bf16[16,19,4096]{2,1,0:T(8,128)(2,1)} copy-done((bf16[16,19,4096]{2,1,0:T(8,128)(2,1)}, bf16[16,19,4096]{2,1,0:T(8,128)(2,1)S(1)}, u32[]{:S(2)}) %copy-start) | copy-done | bytes 2490392
  49.9 4.5 %all-to-all-done.incoming_ref = bf16[32,19,512]{2,1,0:T(8,128)(2,1)S(1)} async-done(((bf16[32,19,512]{2,1,0:T(8,128)(2,1)}), bf16[32,19,512]{2,1,0:T(8,128)(2,1)S(1)}, u32[]{:S(2)}, u32[]{:S(2)}) %all-to-all-start) | async-done | bytes 622624 | tf_op jit(solution)/shard_map/all_to_all | solution.py:596
  54.4 0.0 copy-start.5
  54.4 0.9 %copy-done.5 = bf16[32,19,512]{2,1,0:T(8,128)(2,1)} copy-done((bf16[32,19,512]{2,1,0:T(8,128)(2,1)}, bf16[32,19,512]{2,1,0:T(8,128)(2,1)S(1)}, u32[]{:S(2)}) %copy-start.5) | copy-done | bytes 622616
  55.3 8.0 %fill.1 = bf16[19,24,4096]{2,1,0:T(8,128)(2,1)} custom-call(s32[24]{0:T(128)} %fusion.8.source_ref, s32[16]{0:T(128)} %and_select_fusion.origin_ref, s32[16]{0:T(128)} %get-tuple-element.7.kind_ref, bf16[16,19,4096]{2,1,0:T(8,128)(2,1)} %copy-done, bf16[32,19,512]{2,1,0:T(8,128)(2,1)} %copy-done.5, bf16[256,512]{1,0:T(8,128)(2,1)} %constant.63.clone.spread_ref), custom_call_target="tpu_custom_call" | custom-call | tf_op jit(solution)/shard_map/fill/pallas_call | solution.py:524
  (3 shorter events, 0.0 us)
Async XLA Ops:
  2.8 1.7 %copy-start.1 = (bf16[19,16,32,128]{3,2,1,0:T(8,128)(2,1)S(1)}, bf16[19,16,32,128]{3,2,1,0:T(8,128)(2,1)}, u32[]{:S(2)}) copy-start(bf16[19,16,32,128]{3,2,1,0:T(8,128)(2,1)} %pop_ref.1) | copy-start | bytes 7471108
  4.5 19.4 %copy-start.2 = (bf16[1024,1024]{1,0:T(8,128)(2,1)S(1)}, bf16[1024,1024]{1,0:T(8,128)(2,1)}, u32[]{:S(2)}) copy-start(bf16[1024,1024]{1,0:T(8,128)(2,1)} %constant.61.clone.select_ref) | copy-start | bytes 6291460
  4.5 19.4 %copy-start.3 = (bf16[512,128]{1,0:T(8,128)(2,1)S(1)}, bf16[512,128]{1,0:T(8,128)(2,1)}, u32[]{:S(2)}) copy-start(bf16[512,128]{1,0:T(8,128)(2,1)} %constant.60.clone.shrink_ref) | copy-start | bytes 393220
  23.9 9.6 %copy-start.6 = (s32[512]{0:T(512)S(1)}, s32[512]{0:T(512)}, u32[]{:S(2)}) copy-start(s32[512]{0:T(512)} %param.11) | copy-start | bytes 6148
  24.0 9.8 %copy-start.7 = (s32[512]{0:T(512)S(1)}, s32[512]{0:T(512)}, u32[]{:S(2)}) copy-start(s32[512]{0:T(512)} %param.10) | copy-start | bytes 6148
  28.3 26.1 %all-to-all-start = ((bf16[32,19,512]{2,1,0:T(8,128)(2,1)}), bf16[32,19,512]{2,1,0:T(8,128)(2,1)S(1)}, u32[]{:S(2)}, u32[]{:S(2)}) async-start(bf16[32,19,512]{2,1,0:T(8,128)(2,1)} %merge.1), calls=%async_computation | async-start | bytes 1572864 | tf_op jit(solution)/shard_map/all_to_all | solution.py:596
  35.9 1.6 %copy-start.4 = (bf16[1024,1024]{1,0:T(8,128)(2,1)S(1)}, bf16[1024,1024]{1,0:T(8,128)(2,1)}, u32[]{:S(2)}) copy-start(bf16[1024,1024]{1,0:T(8,128)(2,1)} %constant.62.clone.select_ref) | copy-start | bytes 6291460
  48.2 1.7 %copy-start = (bf16[16,19,4096]{2,1,0:T(8,128)(2,1)}, bf16[16,19,4096]{2,1,0:T(8,128)(2,1)S(1)}, u32[]{:S(2)}) copy-start(bf16[16,19,4096]{2,1,0:T(8,128)(2,1)S(1)} %layout.1.pool_source) | copy-start | bytes 7471108
  54.4 0.9 %copy-start.5 = (bf16[32,19,512]{2,1,0:T(8,128)(2,1)}, bf16[32,19,512]{2,1,0:T(8,128)(2,1)S(1)}, u32[]{:S(2)}) copy-start(bf16[32,19,512]{2,1,0:T(8,128)(2,1)S(1)} %all-to-all-done.incoming_ref) | copy-start | bytes 1867780
